TPU v7x, 32 devices: a whole 2x2x4 slice. The times are simulated.
32 devices in a mesh: qrow: 2 (over x), kcol: 16 (over z, y, core).
Axes of the slice: x: 2, y: 2, z: 4, core: 2. Of those that a mesh axis runs over, the one named last changes fastest.
Arguments:
- queries: bfloat16 [32, 2048], P(('qrow', 'kcol')), may hold values from -96 to 96, as said below
- key_maps: bfloat16 [8192, 2048], P(('qrow', 'kcol')), may hold values from -4.1 to 4.1, as said below
- values: bfloat16 [8192, 2048], P(('qrow', 'kcol')), may hold values from -24 to 24
- lambdas: float32 [8], replicated, may hold values from 0.2 to 0.8
- norm_gain: float32 [2048], replicated, may hold values from 0.1 to 1.9
Outputs:
- attended: bfloat16 [32, 2048], P(('qrow', 'kcol'))
Inputs may be any that keep to these rules, and one draw needn't show every extreme that they name: `queries`: query features of order one in most rows. `key_maps`: key features of order one.
All inputs are finite; a program needn't handle non-finite values.
Results may differ from a plain program's by a relative error of at most 0.014.
Values may be sent and summed in bfloat16 or wider, within the bound.
A program may use at most 64 MiB of HBM per device.

v0:
```python
import math

import jax
import jax.numpy as jnp
from jax import lax
from jax.sharding import PartitionSpec as P


def combined_all(array, axis, combine):
    everything = jax.tree.map(lambda part: lax.all_gather(part, axis), array)
    leading = jax.tree.map(lambda part: part[0], everything)

    def lap(k, so_far):
        return combine(so_far, jax.tree.map(lambda part: part[k], everything))

    return lax.fori_loop(1, lax.axis_size(axis), lap, leading)


def combine_states(first, second):
    max_one, total_one, accum_one = first
    max_two, total_two, accum_two = second
    largest = jnp.maximum(max_one, max_two)
    factor_one = jnp.exp(max_one - largest)
    factor_two = jnp.exp(max_two - largest)
    totals = total_one * factor_one + total_two * factor_two
    accums = accum_one * factor_one[..., None] + accum_two * factor_two[..., None]
    return (largest, totals, accums)


def shards(queries, key_maps, values, lambdas, norm_gain):
    row_count = lax.axis_size("qrow")
    col_count = lax.axis_size("kcol")
    row_index = lax.axis_index("qrow")
    col_index = lax.axis_index("kcol")
    query_dev = queries.shape[0]
    key_dev = key_maps.shape[0]
    head_count = lambdas.shape[0]
    head_width = key_maps.shape[1] // (2 * head_count)
    value_width = values.shape[1] // head_count
    total_keys = key_dev * row_count * col_count
    total_queries = query_dev * row_count * col_count
    scaling = 1.0 / math.sqrt(head_width)
    row_block = lax.all_gather(queries, "kcol", axis=0, tiled=True)
    row_size = row_block.shape[0]
    query_pos = (
        total_keys - total_queries + row_index * row_size + jnp.arange(row_size, dtype=jnp.int32)
    )
    run_max = jnp.full((2, row_size, head_count), -1e30, jnp.float32)
    key_piece = lax.all_gather(key_maps, "qrow", axis=0, tiled=True)
    value_piece = lax.all_gather(values, "qrow", axis=0, tiled=True)
    count = key_piece.shape[0]
    global_row = jnp.arange(count, dtype=jnp.int32)
    key_pos = (global_row // key_dev * col_count + col_index) * key_dev + global_row % key_dev
    visible = key_pos[None, :] <= query_pos[:, None]
    new_max = []
    new_total = []
    new_accum = []
    for map_side in range(2):
        side_max, side_total, side_accum = ([], [], [])
        for head_index in range(head_count):
            lower = (head_index * 2 + map_side) * head_width
            score = (
                lax.dot_general(
                    row_block[:, lower : lower + head_width],
                    key_piece[:, lower : lower + head_width],
                    (((1,), (1,)), ((), ())),
                    preferred_element_type=jnp.float32,
                )
                * scaling
            )
            score = jnp.where(visible, score, -1e30)
            before = run_max[map_side, :, head_index]
            largest = jnp.maximum(before, jnp.max(score, axis=1))
            expo = jnp.where(visible, jnp.exp(score - largest[:, None]), 0.0)
            side_total.append(jnp.sum(expo, axis=1))
            product = jnp.dot(
                expo.astype(jnp.bfloat16),
                value_piece[:, head_index * value_width : (head_index + 1) * value_width],
                preferred_element_type=jnp.float32,
            )
            side_accum.append(product)
            side_max.append(largest)
        new_max.append(jnp.stack(side_max, axis=1))
        new_total.append(jnp.stack(side_total, axis=1))
        new_accum.append(jnp.stack(side_accum, axis=1))
    part_max = jnp.stack(new_max)
    part_total = jnp.stack(new_total)
    part_accum = jnp.stack(new_accum)
    merged = combined_all((part_max, part_total, part_accum), "kcol", combine_states)
    outputs = merged[2] / merged[1][..., None]
    whole_diff = outputs[0] - lambdas[None, :, None] * outputs[1]
    own_diff = lax.dynamic_slice_in_dim(whole_diff, col_index * query_dev, query_dev, 0)
    meansq = jnp.mean(own_diff * own_diff, axis=-1, keepdims=True)
    normed = own_diff / jnp.sqrt(meansq + 1e-05) * norm_gain.reshape(head_count, value_width)
    return normed.reshape(query_dev, head_count * value_width).astype(jnp.bfloat16)


def solution(mesh):
    in_specs = (
        P(("qrow", "kcol"), None),
        P(("qrow", "kcol"), None),
        P(("qrow", "kcol"), None),
        P(),
        P(),
    )
    out_specs = P(("qrow", "kcol"), None)
    return jax.shard_map(shards, mesh=mesh, in_specs=in_specs, out_specs=out_specs, check_vma=False)
```

profile of v0, /device:TPU:0, one launch (start us, length us, event | category | flops | bytes accessed | tf_op | source)
XLA Modules:
  0.0 170.1 jit_solution(10868185162852134317)
XLA Ops:
  6.5 0.7 all-gather.8.cloned.1.call-update
  7.3 0.7 all-gather.10.cloned.1.call-update
  8.1 23.4 %all-gather.3 = bf16[16,1,2048]{2,1,0:T(2,128)(2,1)S(1)} all-gather(bf16[1,1,2048]{2,1,0:T(2,128)(2,1)S(1)} %bitcast.176), channel_id=1, replica_groups=mesh['qrow'=2,'kcol'=16] {'kcol'}, dimensions={0}, use_global_device_ids=true | all-gather | bytes 69632 | tf_op jit(solution)/shard_map/all_gather | solution.py:43
  31.5 0.7 copy.23
  32.2 12.5 %all-gather.8.cloned.1.call-done = bf16[512,2048]{1,0:T(8,128)(2,1)} async-done(((bf16[256,2048]{1,0:T(8,128)(2,1)}), bf16[512,2048]{1,0:T(8,128)(2,1)}) %all-gather.8.cloned.1.call-update) | async-done | bytes 2097168 | tf_op jit(solution)/shard_map/all_gather | solution.py:49
  44.7 1.2 fusion.247
  45.9 1.2 fusion.246
  47.1 1.2 fusion.245
  48.3 1.2 fusion.244
  49.5 1.2 fusion.243
  50.6 1.2 fusion.242
  51.8 1.2 fusion.241
  53.0 1.2 fusion.240
  54.2 1.2 fusion.255
  55.4 1.2 fusion.254
  56.6 1.2 fusion.253
  57.8 1.2 fusion.252
  59.0 1.2 fusion.251
  60.1 1.2 fusion.250
  61.3 1.2 fusion.249
  62.5 1.2 fusion.248
  63.7 15.8 %all-gather.10.cloned.1.call-done = bf16[512,2048]{1,0:T(8,128)(2,1)} async-done(((bf16[256,2048]{1,0:T(8,128)(2,1)}), bf16[512,2048]{1,0:T(8,128)(2,1)}) %all-gather.10.cloned.1.call-update) | async-done | bytes 2097168 | tf_op jit(solution)/shard_map/all_gather | solution.py:50
  79.5 1.3 fusion.34
  80.8 1.1 fusion.26
  81.9 1.1 fusion.33
  83.1 1.1 fusion.32
  84.2 1.1 fusion.31
  85.4 1.1 fusion.30
  86.5 1.1 fusion.29
  87.7 0.2 fusion.28
  87.9 0.2 fusion.27
  88.1 0.2 fusion.25
  88.3 0.2 fusion.24
  88.5 0.2 fusion.23
  88.7 0.2 fusion.22
  88.9 0.2 fusion.21
  89.1 0.2 fusion.20
  89.3 0.2 fusion.19
  89.5 0.8 copy.18
  90.4 0.3 fusion.82
  90.7 0.3 fusion.80
  91.1 22.1 %all-gather.1 = f32[32,16,8]{1,2,0:T(8,128)S(1)} all-gather(f32[2,16,8]{1,2,0:T(8,128)S(1)} %pad_maximum_fusion.2), channel_id=3, replica_groups=mesh['qrow'=2,'kcol'=16] {'kcol'}, dimensions={0}, use_global_device_ids=true | all-gather | bytes 17408 | tf_op jit(solution)/shard_map/all_gather | solution.py:10
  113.2 18.4 %all-gather = f32[32,16,8]{1,2,0:T(8,128)S(1)} all-gather(f32[2,16,8]{1,2,0:T(8,128)S(1)} %pad_maximum_fusion.1), channel_id=2, replica_groups=mesh['qrow'=2,'kcol'=16] {'kcol'}, dimensions={0}, use_global_device_ids=true | all-gather | bytes 17408 | tf_op jit(solution)/shard_map/all_gather | solution.py:10
  131.6 10.4 %all-gather.12.cloned.1.call-done = f32[32,16,8,256]{3,2,1,0:T(8,128)} async-done(((f32[2,16,8,256]{3,2,1,0:T(8,128)}), f32[32,16,8,256]{3,2,1,0:T(8,128)}) %all-gather.12.cloned.1.call-update) | async-done | bytes 4194320 | tf_op jit(solution)/shard_map/all_gather | solution.py:10
  142.0 1.0 slice.233
  143.0 19.4 %while.19 = (s32[]{:T(128)}, f32[2,16,8]{1,2,0:T(8,128)S(1)}, f32[2,16,8]{1,2,0:T(8,128)S(1)}, f32[2,16,8,256]{3,2,1,0:T(8,128)S(1)}, f32[16,2,16,8]{2,3,1,0:T(8...) while((s32[]{:T(128)}, f32[2,16,8]{1,2,0:T(8,128)S(1)}, ...), condition=%wide.region_33.34_spmd, body=%wide.region_32.33_spmd.sunk | while | flops 198149 | bytes 800911 | solution.py:16
  143.2 1.1 fusion.259
  144.5 1.1 fusion.259
  145.8 1.1 fusion.259
  147.1 1.1 fusion.259
  148.4 1.1 fusion.259
  149.7 1.1 fusion.259
  150.9 1.1 fusion.259
  152.2 1.1 fusion.259
  153.5 1.1 fusion.259
  154.8 1.1 fusion.259
  156.1 1.1 fusion.259
  157.4 1.1 fusion.259
  158.7 1.1 fusion.259
  160.0 1.1 fusion.259
  161.3 1.1 fusion.259
  162.5 0.1 broadcast_divide_fusion
  162.6 0.2 multiply_reduce_fusion
  162.9 0.6 copy.21
  (81 shorter events, 2.9 us)
Async XLA Ops:
  6.5 1.6 copy-start
  6.5 38.2 %all-gather.8.cloned.1.call-start = ((), (), s32[]{:S(2)}) async-start(), calls=%async_computation | async-start | bytes 3145728 | tf_op jit(solution)/shard_map/all_gather | solution.py:49
  7.3 72.2 %all-gather.10.cloned.1.call-start = ((), (), s32[]{:S(2)}) async-start(), calls=%async_computation.1 | async-start | bytes 3145728 | tf_op jit(solution)/shard_map/all_gather | solution.py:50
  8.0 134.0 %all-gather.12.cloned.1.call-start = ((), (), s32[]{:S(2)}) async-start(), calls=%async_computation.2 | async-start | bytes 4456448 | tf_op jit(solution)/shard_map/all_gather | solution.py:10
  79.5 8.2 %copy-start.3 = (bf16[512,2048]{1,0:T(8,128)(2,1)S(1)}, bf16[512,2048]{1,0:T(8,128)(2,1)}, u32[]{:S(2)}) copy-start(bf16[512,2048]{1,0:T(8,128)(2,1)} %all-gather.10.cloned.1.call-done) | copy-start | bytes 6291460
  87.9 2.5 %copy-start.1 = (f32[2048]{0:T(1024)S(1)}, f32[2048]{0:T(1024)}, u32[]{:S(2)}) copy-start(f32[2048]{0:T(1024)} %param.11) | copy-start | bytes 24580
  143.0 19.6 %copy-start.2 = (f32[8]{0:T(128)S(1)}, f32[8]{0:T(128)}, u32[]{:S(2)}) copy-start(f32[8]{0:T(128)} %param.10) | copy-start | bytes 100
Sparse Core Ops, SparseCore 0:
  8.9 35.8 all-gather.7
  46.3 33.1 all-gather.9
  90.5 51.4 all-gather.11
where the time goes:
time: 171 us; the launch traced here: 170 us
  blocking collectives  63.9 us (37%)
  waiting for transfers between devices  40.2 us (24%)
  matrix products  28.7 us (17%)
  other arithmetic  17.9 us (10%)
  between operations  13.4 us (8%)
  local copies, waits for them, and re-layouts  5.49 us (3%)
    all_gather x2, blocking collectives, combined_all(): everything = jax.tree.map(lambda part: lax.all_gather(part, axis), array)  40.5 us
    all_gather x1, blocking collectives, shards(): row_block = lax.all_gather(queries, 'kcol', axis=0, tiled=True)  23.4 us
    dot_general x16, matrix products, shards(): lax.dot_general(row_block[:, lower:lower + head_width], key_piece[:, lowe...  18.8 us
    add x15, other arithmetic, combine_states(): accum_one * factor_one[..., None] + accum_two * factor_two[..., None]  16.5 us
    all_gather x1, waiting for transfers between devices, shards(): value_piece = lax.all_gather(values, 'qrow', axis=0, tiled=True)  15.8 us
    all_gather x1, waiting for transfers between devices, shards(): key_piece = lax.all_gather(key_maps, 'qrow', axis=0, tiled=True)  12.5 us
    all_gather x1, waiting for transfers between devices, combined_all(): everything = jax.tree.map(lambda part: lax.all_gather(part, axis), array)  10.4 us
    dot_general x16, matrix products, shards(): jnp.dot(expo.astype(jnp.bfloat16), value_piece[:, head_index * value_widt...  9.95 us
  transfers between devices with their start and end apart: 3, of which 3 were waited for; matrix products, arithmetic and copies ran while one was open for 12% of the time, Pallas kernels for 0%

commit v1 on v0

v1 whole, which is shorter than its diff:
```python
import functools
import math

import jax
import jax.numpy as jnp
from jax import lax
from jax.experimental import pallas as pl
from jax.experimental.pallas import tpu as pltpu
from jax.sharding import PartitionSpec as P

MESH = pl.DeviceIdType.MESH
LOWEST = -1e30


def kernel(
    rows, cols, key_dev, heads,
    q_hbm, k_hbm, v_hbm, lam_ref, gain_hbm,
    out_ref,
    q_own, gain_own, k_buf, v_buf, q_split, q_pair, q_all, q_wide,
    part_wide, part_send, part_recv, diff_pad, gain_rows, fin_send, fin_recv,
    q_sem, gain_sem, k_own_sem, v_own_sem, k_send, k_recv, v_send, v_recv,
    qx_send, qx_recv, qa_send, qa_recv, pa_send, pa_recv, fx_send, fx_recv,
):
    row = lax.axis_index("qrow")
    col = lax.axis_index("kcol")
    core = lax.rem(col, 2)
    half_cols = cols // 2
    pairs = rows * half_cols
    pair = row * half_cols + lax.div(col, 2)
    sib = (row, col + 1 - 2 * core)
    group = heads // 2
    maps = 2 * group
    width = group * 256
    tall = 2 * pairs

    def peer(offset):
        other = lax.rem(pair + offset, pairs)
        return (lax.div(other, half_cols), 2 * lax.rem(other, half_cols) + core)

    def columns(which, h):
        return pl.ds(pl.multiple_of(which * width + h * 256, 128), 256)

    q_copy = pltpu.make_async_copy(q_hbm, q_own, q_sem)
    q_copy.start()
    gain_copy = pltpu.make_async_copy(gain_hbm, gain_own, gain_sem)
    gain_copy.start()
    k_locals, v_locals = [], []
    for h in range(group):
        k_locals.append(pltpu.make_async_copy(
            k_hbm.at[:, columns(core, h)], k_buf.at[h, pl.ds(0, key_dev)], k_own_sem.at[h]))
        k_locals[-1].start()
    for h in range(group):
        v_locals.append(pltpu.make_async_copy(
            v_hbm.at[:, columns(core, h)], v_buf.at[h, pl.ds(0, key_dev)], v_own_sem.at[h]))
        v_locals[-1].start()

    barrier = pltpu.get_barrier_semaphore()
    pl.semaphore_signal(barrier, inc=1, device_id=sib, device_id_type=MESH)

    def greet(i, carry):
        pl.semaphore_signal(barrier, inc=1, device_id=peer(i), device_id_type=MESH)
        return carry

    lax.fori_loop(1, pairs, greet, 0)

    q_copy.wait()
    for g in range(2):
        for m in range(maps):
            at = (g * maps + m) * 128
            q_split[g, m : m + 1, :] = q_own[:, at : at + 128].astype(jnp.float32)
    q_pair[core] = q_split[core]

    pl.semaphore_wait(barrier, pairs)

    q_cross = pltpu.make_async_remote_copy(
        src_ref=q_split.at[1 - core], dst_ref=q_pair.at[core], send_sem=qx_send, recv_sem=qx_recv,
        device_id=sib, device_id_type=MESH)
    q_cross.start()
    k_cross, v_cross = [], []
    for h in range(group):
        k_cross.append(pltpu.make_async_remote_copy(
            src_ref=k_hbm.at[:, columns(1 - core, h)], dst_ref=k_buf.at[h, pl.ds(key_dev, key_dev)],
            send_sem=k_send.at[h], recv_sem=k_recv.at[h], device_id=sib, device_id_type=MESH))
        k_cross[-1].start()
    for h in range(group):
        v_cross.append(pltpu.make_async_remote_copy(
            src_ref=v_hbm.at[:, columns(1 - core, h)], dst_ref=v_buf.at[h, pl.ds(key_dev, key_dev)],
            send_sem=v_send.at[h], recv_sem=v_recv.at[h], device_id=sib, device_id_type=MESH))
        v_cross[-1].start()

    q_cross.wait_recv()
    q_all[0] = q_pair[...].reshape(2 * maps, 128).astype(jnp.bfloat16)

    def send_query(i, carry):
        pltpu.make_async_remote_copy(
            src_ref=q_all.at[0], dst_ref=q_all.at[pairs - i], send_sem=qa_send, recv_sem=qa_recv,
            device_id=peer(i), device_id_type=MESH).start()
        return carry

    lax.fori_loop(1, pairs, send_query, 0)

    gain_copy.wait()
    for part in range(2):
        for h in range(group):
            line = gain_own[pl.ds((core * group + h) * 2 + part, 1), :]
            gain_rows[part, h : h + 1, :] = line
            gain_rows[part, group + h : group + h + 1, :] = line
    line_of = lax.rem(lax.broadcasted_iota(jnp.int32, (2 * group, 128), 0), group)
    lam = jnp.zeros((2 * group, 128), jnp.float32)
    for h in range(group):
        lam = jnp.where(line_of == h, lam_ref[core * group + h], lam)

    keys = 2 * key_dev
    row_of = lax.broadcasted_iota(jnp.int32, (tall, keys), 0)
    col_of = lax.broadcasted_iota(jnp.int32, (tall, keys), 1)
    query = 2 * pair + row_of
    query = jnp.where(query >= tall, query - tall, query)
    block = jnp.where(col_of < key_dev, 2 * pair + core, 2 * pair + 1 - core)
    place = jnp.where(col_of < key_dev, col_of, col_of - key_dev)
    visible = block * key_dev + place <= tall * key_dev - tall + query
    lane = lax.broadcasted_iota(jnp.int32, (tall, 128), 1)
    scaling = 1.0 / math.sqrt(128)

    pltpu.make_async_copy(q_all.at[pl.ds(1, pairs - 1)], q_all.at[pl.ds(1, pairs - 1)], qa_recv).wait()
    q_wide[...] = q_all[...].reshape(pairs * 2 * maps, 128).astype(jnp.float32)

    for h in range(group):
        k_locals[h].wait()
        k_cross[h].wait_recv()
        expos = []
        for side in range(2):
            m = 2 * h + side
            q_map = q_wide[pl.ds(m, tall, stride=maps), :].astype(jnp.bfloat16)
            score = lax.dot_general(
                q_map, k_buf[h, :, side * 128 : side * 128 + 128], (((1,), (1,)), ((), ())),
                preferred_element_type=jnp.float32) * scaling
            score = jnp.where(visible, score, LOWEST)
            top = jnp.max(score, axis=1, keepdims=True).astype(jnp.bfloat16).astype(jnp.float32)
            expo = jnp.where(visible, jnp.exp(score - top), 0.0)
            total = jnp.sum(expo, axis=1, keepdims=True)
            high = total.astype(jnp.bfloat16).astype(jnp.float32)
            stats = jnp.where(lane == 0, top, jnp.where(lane == 1, high, total - high))
            part_wide[2, pl.ds(m, tall, stride=maps), :] = stats
            expos.append(expo.astype(jnp.bfloat16))
        v_locals[h].wait()
        v_cross[h].wait_recv()
        summed = jnp.dot(jnp.concatenate(expos, axis=0), v_buf[h], preferred_element_type=jnp.float32)
        for side in range(2):
            for part in range(2):
                part_wide[part, pl.ds(2 * h + side, tall, stride=maps), :] = summed[
                    side * tall : (side + 1) * tall, part * 128 : part * 128 + 128]

    for part in range(3):
        part_send[:, part] = part_wide[part].reshape(pairs, 2 * maps, 128).astype(jnp.bfloat16)

    def send_part(i, carry):
        pltpu.make_async_remote_copy(
            src_ref=part_send.at[i], dst_ref=part_recv.at[i], send_sem=pa_send, recv_sem=pa_recv,
            device_id=peer(i), device_id_type=MESH).start()
        return carry

    lax.fori_loop(1, pairs, send_part, 0)
    part_recv[0] = part_send[0]
    pltpu.make_async_copy(
        part_recv.at[pl.ds(1, pairs - 1)], part_recv.at[pl.ds(1, pairs - 1)], pa_recv).wait()

    stats_all = part_recv[:, 2].astype(jnp.float32)
    peak = jnp.max(stats_all, axis=0)
    shape = (2 * maps, 128)
    sums = [jnp.zeros(shape, jnp.float32) for _ in range(3)]
    for s in range(pairs):
        factor = jnp.broadcast_to(jnp.exp(stats_all[s] - peak)[:, 0:1], shape)
        for part in range(3):
            sums[part] = sums[part] + factor * part_recv[s, part].astype(jnp.float32)
    totals = sums[2][:, 1:2] + sums[2][:, 2:3]
    diffs = []
    for part in range(2):
        diff_pad[part] = sums[part] / totals
        diffs.append(
            diff_pad[part, pl.ds(0, maps, stride=2), :] - lam * diff_pad[part, pl.ds(1, maps, stride=2), :])
    square = jnp.sum(diffs[0] * diffs[0] + diffs[1] * diffs[1], axis=1, keepdims=True) * (1.0 / 256)
    scale = jnp.sqrt(square + 1e-05)
    for part in range(2):
        normed = diffs[part] / scale * gain_rows[part]
        for j in range(2):
            fin_send[j, part * group : (part + 1) * group, :] = normed[j * group : (j + 1) * group]
    fin_cross = pltpu.make_async_remote_copy(
        src_ref=fin_send.at[1 - core], dst_ref=fin_recv, send_sem=fx_send, recv_sem=fx_recv,
        device_id=sib, device_id_type=MESH)
    fin_cross.start()

    def put(which, lines):
        for part in range(2):
            for h in range(group):
                at = pl.ds(pl.multiple_of(which * width + h * 256 + part * 128, 128), 128)
                out_ref[:, at] = lines[part * group + h : part * group + h + 1]

    put(core, fin_send[core])
    q_cross.wait_send()
    for h in range(group):
        k_cross[h].wait_send()
        v_cross[h].wait_send()
    pltpu.make_async_copy(q_all.at[pl.ds(1, pairs - 1)], q_all.at[pl.ds(1, pairs - 1)], qa_send).wait()
    pltpu.make_async_copy(
        part_send.at[pl.ds(1, pairs - 1)], part_send.at[pl.ds(1, pairs - 1)], pa_send).wait()
    fin_cross.wait()
    put(1 - core, fin_recv[...])


def shards(queries, key_maps, values, lambdas, norm_gain):
    rows, cols = lax.axis_size("qrow"), lax.axis_size("kcol")
    heads = lambdas.shape[0]
    key_dev = key_maps.shape[0]
    assert queries.shape[0] == 1 and heads == 8
    assert key_maps.shape[1] == 2048 and values.shape[1] == 2048
    assert cols % 2 == 0
    group = heads // 2
    maps = 2 * group
    pairs = rows * cols // 2
    tall = 2 * pairs
    f32, bf16 = jnp.float32, jnp.bfloat16
    dma = pltpu.SemaphoreType.DMA
    anywhere = pl.BlockSpec(memory_space=pl.ANY)
    out = pl.pallas_call(
        functools.partial(kernel, rows, cols, key_dev, heads),
        out_shape=jax.ShapeDtypeStruct((1, 2048), f32),
        in_specs=[anywhere, anywhere, anywhere, pl.BlockSpec(memory_space=pltpu.SMEM), anywhere],
        out_specs=pl.BlockSpec(memory_space=pltpu.VMEM),
        scratch_shapes=[
            pltpu.VMEM((1, 2048), bf16),
            pltpu.VMEM((16, 128), f32),
            pltpu.VMEM((group, 2 * key_dev, 256), bf16),
            pltpu.VMEM((group, 2 * key_dev, 256), bf16),
            pltpu.VMEM((2, maps, 128), f32),
            pltpu.VMEM((2, maps, 128), f32),
            pltpu.VMEM((pairs, 2 * maps, 128), bf16),
            pltpu.VMEM((pairs * 2 * maps, 128), f32),
            pltpu.VMEM((3, pairs * 2 * maps, 128), f32),
            pltpu.VMEM((pairs, 3, 2 * maps, 128), bf16),
            pltpu.VMEM((pairs, 3, 2 * maps, 128), bf16),
            pltpu.VMEM((2, 2 * maps, 128), f32),
            pltpu.VMEM((2, 2 * group, 128), f32),
            pltpu.VMEM((2, 2 * group, 128), f32),
            pltpu.VMEM((2 * group, 128), f32),
            dma, dma, dma((group,)), dma((group,)), dma((group,)), dma((group,)), dma((group,)), dma((group,)),
            dma, dma, dma, dma, dma, dma, dma, dma,
        ],
        compiler_params=pltpu.CompilerParams(
            collective_id=0, has_side_effects=True, vmem_limit_bytes=40 * 2**20),
        cost_estimate=pl.CostEstimate(
            flops=6 * tall * 2 * key_dev * 1024, bytes_accessed=4 * key_dev * 2048, transcendentals=0),
    )(queries, key_maps, values, lambdas, norm_gain.reshape(16, 128))
    return out.astype(bf16)


def solution(mesh):
    in_specs = (
        P(("qrow", "kcol"), None),
        P(("qrow", "kcol"), None),
        P(("qrow", "kcol"), None),
        P(),
        P(),
    )
    out_specs = P(("qrow", "kcol"), None)
    return jax.shard_map(shards, mesh=mesh, in_specs=in_specs, out_specs=out_specs, check_vma=False)
```

time: 171 us -> 27.9 us (0.16)
  blocking collectives: 63.9 us -> 0 us
  waiting for transfers between devices: 40.2 us -> 0 us
  matrix products: 28.7 us -> 0 us
  Pallas kernels: 0 us -> 22.5 us
  other arithmetic: 17.9 us -> 0.61 us
  between operations: 13.4 us -> 0.01 us
    all_gather x3 -> x0, blocking collectives: 63.9 us -> none  [the longest x2 40.5 us: combined_all(): everything = jax.tree.map(lambda part: lax.all_gather(part, axis), array)]
    all_gather x3 -> x0, waiting for transfers between devices: 38.7 us -> none  [the longest x1 15.8 us: shards(): value_piece = lax.all_gather(values, 'qrow', axis=0, tiled=True)]
    dot_general x32 -> x0, matrix products: 28.7 us -> none  [the longest x16 18.8 us: shards(): lax.dot_general(row_block[:, lower:lower + head_width], key_piece[:, lowe...]
    pallas_call x0 -> x1, Pallas kernels: none -> 22.5 us  [shards(): pl.pallas_call(functools.partial(kernel, rows, cols, key_dev, heads), out...]
    add x32 -> x0, other arithmetic: 16.8 us -> none  [the longest x15 16.5 us: combine_states(): accum_one * factor_one[..., None] + accum_two * factor_two[..., None]]
    unnamed x10, local copies, waits for them, and re-layouts: 1.31 us -> 4.5 us
    exp x30 -> x0, local copies, waits for them, and re-layouts: 2.16 us -> none  [the longest x15 1.09 us: combine_states(): factor_two = jnp.exp(max_two - largest)]
  transfers between devices with their start and end apart: 3 -> 0, of which waited for: 3 -> 0; matrix products, arithmetic and copies ran while one was open for 12% -> 0% of each run, Pallas kernels for 0% -> 0%
where the time goes in v1:
time: 27.9 us; the launch traced here: 27.7 us
  Pallas kernels  22.5 us (81%)
  local copies, waits for them, and re-layouts  4.5 us (16%)
  other arithmetic  0.61 us (2%)
    pallas_call x1, Pallas kernels, shards(): pl.pallas_call(functools.partial(kernel, rows, cols, key_dev, heads), out...  22.5 us
    unnamed x10, local copies, waits for them, and re-layouts  4.5 us
    convert_element_type x1, other arithmetic, shards(): return out.astype(bf16)  0.61 us

profile of v1, /device:TPU:0, one launch (start us, length us, event | category | flops | bytes accessed | tf_op | source)
XLA Modules:
  0.0 27.7 jit_solution(8207553530863418936)
XLA Ops:
  0.0 0.0 copy-start.4
  0.0 0.7 %copy-done.4 = f32[8]{0:T(128)S(1)} copy-done((f32[8]{0:T(128)S(1)}, f32[8]{0:T(128)}, u32[]{:S(2)}) %copy-start.4) | copy-done | bytes 56
  0.7 0.0 copy-start
  0.7 1.2 %copy-done = bf16[256,2048]{1,0:T(8,128)(2,1)S(1)} copy-done((bf16[256,2048]{1,0:T(8,128)(2,1)S(1)}, bf16[256,2048]{1,0:T(8,128)(2,1)}, u32[]{:S(2)}) %copy-start) | copy-done | bytes 1048600
  1.9 0.0 copy-start.1
  1.9 1.2 %copy-done.1 = bf16[256,2048]{1,0:T(8,128)(2,1)S(1)} copy-done((bf16[256,2048]{1,0:T(8,128)(2,1)S(1)}, bf16[256,2048]{1,0:T(8,128)(2,1)}, u32[]{:S(2)}) %copy-start.1) | copy-done | bytes 1048600
  3.1 0.0 copy-start.2
  3.1 0.7 %copy-done.2 = bf16[1,2048]{1,0:T(2,128)(2,1)S(1)} copy-done((bf16[1,2048]{1,0:T(2,128)(2,1)S(1)}, bf16[1,2048]{1,0:T(2,128)(2,1)}, u32[]{:S(2)}) %copy-start.2) | copy-done | bytes 4120
  3.8 0.0 copy-start.3
  3.8 0.7 %copy-done.3 = f32[2048]{0:T(1024)S(1)} copy-done((f32[2048]{0:T(1024)S(1)}, f32[2048]{0:T(1024)}, u32[]{:S(2)}) %copy-start.3) | copy-done | bytes 8216
  4.5 22.5 %shard_map.55 = f32[1,2048]{1,0:T(1,128)S(1)} custom-call(bf16[1,2048]{1,0:T(2,128)(2,1)S(1)} %copy-done.2, bf16[256,2048]{1,0:T(8,128)(2,1)S(1)} %copy-done, bf16[256,2048]{1,0:T(8,128)(2,1)S(1)} %copy-done.1, f32[8]{0:T(128)S(1)} %copy-done.4, f32[16,128]{1,0:T(8,128)S(1)} %bitcast.1), custom_call_target="tpu_custom_call" | custom-call | flops 100663296 | bytes 2097152 | tf_op jit(solution)/shard_map/pallas_call | solution.py:224
  27.1 0.6 %convert_element_type.3 = bf16[1,2048]{1,0:T(2,128)(2,1)} convert(f32[1,2048]{1,0:T(1,128)S(1)} %shard_map.55) | non-fusion elementwise | flops 2048 | bytes 12288 | tf_op jit(solution)/shard_map/convert_element_type | solution.py:253
Async XLA Ops:
  0.0 0.7 %copy-start.4 = (f32[8]{0:T(128)S(1)}, f32[8]{0:T(128)}, u32[]{:S(2)}) copy-start(f32[8]{0:T(128)} %lam_ref.1) | copy-start | bytes 100
  0.7 1.2 %copy-start = (bf16[256,2048]{1,0:T(8,128)(2,1)S(1)}, bf16[256,2048]{1,0:T(8,128)(2,1)}, u32[]{:S(2)}) copy-start(bf16[256,2048]{1,0:T(8,128)(2,1)} %k_hbm.1) | copy-start | bytes 3145732
  1.9 1.2 %copy-start.1 = (bf16[256,2048]{1,0:T(8,128)(2,1)S(1)}, bf16[256,2048]{1,0:T(8,128)(2,1)}, u32[]{:S(2)}) copy-start(bf16[256,2048]{1,0:T(8,128)(2,1)} %v_hbm.1) | copy-start | bytes 3145732
  3.1 0.7 %copy-start.2 = (bf16[1,2048]{1,0:T(2,128)(2,1)S(1)}, bf16[1,2048]{1,0:T(2,128)(2,1)}, u32[]{:S(2)}) copy-start(bf16[1,2048]{1,0:T(2,128)(2,1)} %q_hbm.1) | copy-start | bytes 12292
  3.8 0.7 %copy-start.3 = (f32[2048]{0:T(1024)S(1)}, f32[2048]{0:T(1024)}, u32[]{:S(2)}) copy-start(f32[2048]{0:T(1024)} %param.9) | copy-start | bytes 24580

commit v2 on v1

v2 whole, which is shorter than its diff:
```python
import functools
import math

import jax
import jax.numpy as jnp
from jax import lax
from jax.experimental import pallas as pl
from jax.experimental.pallas import tpu as pltpu
from jax.sharding import PartitionSpec as P

MESH = pl.DeviceIdType.MESH
LOWEST = -1e30


def kernel(
    rows, cols, key_dev, heads,
    q_hbm, k_hbm, v_hbm, lam_hbm, gain_hbm,
    out_ref,
    q_own, lam_own, gain_own, k_buf, v_buf, q_split, q_pair, q_all, q_wide, bias,
    stat_send, stat_recv, part_wide, part_send, part_recv, sum_pad, gain_rows, fin_send, fin_recv,
    q_sem, lam_sem, gain_sem, k_own_sem, v_own_sem, k_send, k_recv, v_send, v_recv,
    qx_send, qx_recv, qa_send, qa_recv, st_send, st_recv, pa_send, pa_recv, fx_send, fx_recv,
):
    row = lax.axis_index("qrow")
    col = lax.axis_index("kcol")
    core = lax.rem(col, 2)
    half_cols = cols // 2
    pairs = rows * half_cols
    pair = row * half_cols + lax.div(col, 2)
    sib = (row, col + 1 - 2 * core)
    group = heads // 2
    maps = 2 * group
    width = group * 256
    tall = 2 * pairs
    keys = 2 * key_dev

    def peer(offset):
        other = pair + offset
        other = jnp.where(other >= pairs, other - pairs, other)
        its_row = lax.div(other, half_cols)
        return (its_row, 2 * (other - its_row * half_cols) + core)

    def for_peers(step):
        if pairs <= 16:
            for i in range(1, pairs):
                step(i)
        else:
            lax.fori_loop(1, pairs, lambda i, carry: (step(i), carry)[1], 0)

    def columns(which, h):
        return pl.ds(pl.multiple_of(which * width + h * 256, 128), 256)

    def all_of(ref, sem):
        pltpu.make_async_copy(ref, ref, sem).wait()

    q_copy = pltpu.make_async_copy(q_hbm, q_own, q_sem)
    q_copy.start()
    barrier = pltpu.get_barrier_semaphore()
    for_peers(lambda i: pl.semaphore_signal(barrier, inc=1, device_id=peer(i), device_id_type=MESH))
    pl.semaphore_signal(barrier, inc=1, device_id=sib, device_id_type=MESH)

    lam_copy = pltpu.make_async_copy(lam_hbm, lam_own, lam_sem)
    lam_copy.start()
    gain_copy = pltpu.make_async_copy(gain_hbm, gain_own, gain_sem)
    gain_copy.start()
    k_locals, v_locals = [], []
    for h in range(group):
        k_locals.append(pltpu.make_async_copy(
            k_hbm.at[:, columns(core, h)], k_buf.at[h, pl.ds(0, key_dev)], k_own_sem.at[h]))
        k_locals[-1].start()
    for h in range(group):
        v_locals.append(pltpu.make_async_copy(
            v_hbm.at[:, columns(core, h)], v_buf.at[h, pl.ds(0, key_dev)], v_own_sem.at[h]))
        v_locals[-1].start()

    q_copy.wait()
    for g in range(2):
        for m in range(maps):
            at = (g * maps + m) * 128
            q_split[g, m : m + 1, :] = q_own[:, at : at + 128].astype(jnp.float32)
    q_pair[core] = q_split[core]

    pl.semaphore_wait(barrier, pairs)

    q_cross = pltpu.make_async_remote_copy(
        src_ref=q_split.at[1 - core], dst_ref=q_pair.at[core], send_sem=qx_send, recv_sem=qx_recv,
        device_id=sib, device_id_type=MESH)
    q_cross.start()
    k_cross, v_cross = [], []
    for h in range(group):
        k_cross.append(pltpu.make_async_remote_copy(
            src_ref=k_hbm.at[:, columns(1 - core, h)], dst_ref=k_buf.at[h, pl.ds(key_dev, key_dev)],
            send_sem=k_send.at[h], recv_sem=k_recv.at[h], device_id=sib, device_id_type=MESH))
        k_cross[-1].start()
    for h in range(group):
        v_cross.append(pltpu.make_async_remote_copy(
            src_ref=v_hbm.at[:, columns(1 - core, h)], dst_ref=v_buf.at[h, pl.ds(key_dev, key_dev)],
            send_sem=v_send.at[h], recv_sem=v_recv.at[h], device_id=sib, device_id_type=MESH))
        v_cross[-1].start()

    q_cross.wait_recv()
    q_all[0] = q_pair[...].reshape(2 * maps, 128).astype(jnp.bfloat16)
    for_peers(lambda i: pltpu.make_async_remote_copy(
        src_ref=q_all.at[0], dst_ref=q_all.at[pairs - i], send_sem=qa_send, recv_sem=qa_recv,
        device_id=peer(i), device_id_type=MESH).start())

    gain_copy.wait()
    for part in range(2):
        for h in range(group):
            line = gain_own[pl.ds((core * group + h) * 2 + part, 1), :]
            gain_rows[part, h : h + 1, :] = line
            gain_rows[part, group + h : group + h + 1, :] = line
    lam_copy.wait()
    map_of = lax.broadcasted_iota(jnp.int32, (maps, tall), 0)
    sign = jnp.ones((maps, tall), jnp.float32)
    for h in range(group):
        sign = jnp.where(map_of == 2 * h + 1, -lam_own[core * group + h], sign)

    row_of = lax.broadcasted_iota(jnp.int32, (2 * tall, keys), 0)
    col_of = lax.broadcasted_iota(jnp.int32, (2 * tall, keys), 1)
    query = 2 * pair + jnp.where(row_of < tall, row_of, row_of - tall)
    query = jnp.where(query >= tall, query - tall, query)
    place = jnp.where(
        col_of < key_dev,
        (2 * pair + core) * key_dev + col_of,
        (2 * pair + 1 - core) * key_dev + col_of - key_dev)
    bias[...] = jnp.where(place <= tall * key_dev - tall + query, 0.0, LOWEST)
    lane = lax.broadcasted_iota(jnp.int32, (tall, 128), 1)
    scaling = 1.0 / math.sqrt(128)

    for h in range(group):
        k_locals[h].wait()
        k_cross[h].wait_recv()
    all_of(q_all.at[pl.ds(1, pairs - 1)], qa_recv)
    q_wide[...] = q_all[...].reshape(pairs * 2 * maps, 128).astype(jnp.float32)

    stats = jnp.zeros((tall, 128), jnp.float32)
    expos = []
    blank = jnp.zeros((tall, 128), jnp.bfloat16)
    for h in range(group):
        first = q_wide[pl.ds(2 * h, tall, stride=maps), :].astype(jnp.bfloat16)
        second = q_wide[pl.ds(2 * h + 1, tall, stride=maps), :].astype(jnp.bfloat16)
        both = jnp.concatenate(
            [jnp.concatenate([first, blank], axis=1), jnp.concatenate([blank, second], axis=1)], axis=0)
        score = lax.dot_general(
            both, k_buf[h], (((1,), (1,)), ((), ())), preferred_element_type=jnp.float32)
        score = score * scaling + bias[...]
        top = jnp.max(score, axis=1, keepdims=True)
        expo = jnp.exp(score - top)
        total = jnp.sum(expo, axis=1, keepdims=True)
        for side in range(2):
            m = 2 * h + side
            at = slice(side * tall, (side + 1) * tall)
            stats = jnp.where(lane == m, top[at], jnp.where(lane == maps + m, total[at], stats))
        expos.append(expo.astype(jnp.bfloat16))
    stat_send[...] = stats
    for_peers(lambda i: pltpu.make_async_remote_copy(
        src_ref=stat_send.at[pl.ds(2 * i, 2)], dst_ref=stat_recv.at[pl.ds(2 * i, 2)],
        send_sem=st_send, recv_sem=st_recv, device_id=peer(i), device_id_type=MESH).start())
    stat_recv[0:2] = stat_send[0:2]

    for h in range(group):
        v_locals[h].wait()
        v_cross[h].wait_recv()
    for h in range(group):
        summed = jnp.dot(expos[h], v_buf[h], preferred_element_type=jnp.float32)
        for side in range(2):
            for part in range(2):
                part_wide[part, pl.ds(2 * h + side, tall, stride=maps), :] = summed[
                    side * tall : (side + 1) * tall, part * 128 : part * 128 + 128]
    for part in range(2):
        part_send[:, part] = part_wide[part].reshape(pairs, 2 * maps, 128).astype(jnp.bfloat16)
    for_peers(lambda i: pltpu.make_async_remote_copy(
        src_ref=part_send.at[i], dst_ref=part_recv.at[i], send_sem=pa_send, recv_sem=pa_recv,
        device_id=peer(i), device_id_type=MESH).start())
    part_recv[0] = part_send[0]

    all_of(stat_recv.at[pl.ds(2, tall - 2)], st_recv)
    turned = stat_recv[...].T
    tops, totals = turned[0:maps], turned[maps : 2 * maps]
    even = lax.rem(lax.broadcasted_iota(jnp.int32, (maps, tall), 1), 2) == 0

    def per_query(array, reduce, fill):
        zero = reduce(jnp.where(even, array, fill), axis=1, keepdims=True)
        one = reduce(jnp.where(even, fill, array), axis=1, keepdims=True)
        return jnp.where(even, zero, one)

    factor = jnp.exp(tops - per_query(tops, jnp.max, -3e38))
    factor = factor * sign / per_query(factor * totals, jnp.sum, 0.0)

    all_of(part_recv.at[pl.ds(1, pairs - 1)], pa_recv)
    sums = [[jnp.zeros((maps, 128), jnp.float32) for _ in range(2)] for _ in range(2)]
    for s in range(pairs):
        for part in range(2):
            block = part_recv[s, part].astype(jnp.float32)
            for j in range(2):
                weight = factor[:, 2 * s + j : 2 * s + j + 1]
                sums[part][j] = sums[part][j] + weight * block[j * maps : (j + 1) * maps]
    diffs = []
    for part in range(2):
        for j in range(2):
            sum_pad[part, j * maps : (j + 1) * maps] = sums[part][j]
        diffs.append(
            sum_pad[part, pl.ds(0, maps, stride=2), :] + sum_pad[part, pl.ds(1, maps, stride=2), :])
    square = jnp.sum(diffs[0] * diffs[0] + diffs[1] * diffs[1], axis=1, keepdims=True) * (1.0 / 256)
    scale = jnp.sqrt(square + 1e-05)
    for part in range(2):
        normed = diffs[part] / scale * gain_rows[part]
        for j in range(2):
            fin_send[j, part * group : (part + 1) * group, :] = normed[j * group : (j + 1) * group]
    fin_cross = pltpu.make_async_remote_copy(
        src_ref=fin_send.at[1 - core], dst_ref=fin_recv, send_sem=fx_send, recv_sem=fx_recv,
        device_id=sib, device_id_type=MESH)
    fin_cross.start()

    def put(which, lines):
        for part in range(2):
            for h in range(group):
                at = pl.ds(pl.multiple_of(which * width + h * 256 + part * 128, 128), 128)
                out_ref[:, at] = lines[part * group + h : part * group + h + 1]

    put(core, fin_send[core])
    q_cross.wait_send()
    for h in range(group):
        k_cross[h].wait_send()
        v_cross[h].wait_send()
    all_of(q_all.at[pl.ds(1, pairs - 1)], qa_send)
    all_of(stat_send.at[pl.ds(2, tall - 2)], st_send)
    all_of(part_send.at[pl.ds(1, pairs - 1)], pa_send)
    fin_cross.wait()
    put(1 - core, fin_recv[...])


def shards(queries, key_maps, values, lambdas, norm_gain):
    rows, cols = lax.axis_size("qrow"), lax.axis_size("kcol")
    heads = lambdas.shape[0]
    key_dev = key_maps.shape[0]
    assert queries.shape[0] == 1 and heads == 8
    assert key_maps.shape[1] == 2048 and values.shape[1] == 2048
    assert cols % 2 == 0 and rows * cols <= 2 * key_dev
    group = heads // 2
    maps = 2 * group
    pairs = rows * cols // 2
    tall = 2 * pairs
    f32, bf16 = jnp.float32, jnp.bfloat16
    dma = pltpu.SemaphoreType.DMA
    in_hbm = pl.BlockSpec(memory_space=pltpu.HBM)
    out = pl.pallas_call(
        functools.partial(kernel, rows, cols, key_dev, heads),
        out_shape=jax.ShapeDtypeStruct((1, 2048), f32),
        in_specs=[in_hbm] * 5,
        out_specs=pl.BlockSpec(memory_space=pltpu.VMEM),
        scratch_shapes=[
            pltpu.VMEM((1, 2048), bf16),
            pltpu.SMEM((heads,), f32),
            pltpu.VMEM((16, 128), f32),
            pltpu.VMEM((group, 2 * key_dev, 256), bf16),
            pltpu.VMEM((group, 2 * key_dev, 256), bf16),
            pltpu.VMEM((2, maps, 128), f32),
            pltpu.VMEM((2, maps, 128), f32),
            pltpu.VMEM((pairs, 2 * maps, 128), bf16),
            pltpu.VMEM((pairs * 2 * maps, 128), f32),
            pltpu.VMEM((2 * tall, 2 * key_dev), f32),
            pltpu.VMEM((tall, 128), f32),
            pltpu.VMEM((tall, 128), f32),
            pltpu.VMEM((2, pairs * 2 * maps, 128), f32),
            pltpu.VMEM((pairs, 2, 2 * maps, 128), bf16),
            pltpu.VMEM((pairs, 2, 2 * maps, 128), bf16),
            pltpu.VMEM((2, 2 * maps, 128), f32),
            pltpu.VMEM((2, 2 * group, 128), f32),
            pltpu.VMEM((2, 2 * group, 128), f32),
            pltpu.VMEM((2 * group, 128), f32),
            dma, dma, dma,
            dma((group,)), dma((group,)), dma((group,)), dma((group,)), dma((group,)), dma((group,)),
            dma, dma, dma, dma, dma, dma, dma, dma, dma, dma,
        ],
        compiler_params=pltpu.CompilerParams(
            collective_id=0, has_side_effects=True, vmem_limit_bytes=40 * 2**20),
        cost_estimate=pl.CostEstimate(
            flops=6 * tall * 2 * key_dev * 1024, bytes_accessed=4 * key_dev * 2048, transcendentals=0),
    )(queries, key_maps, values, lambdas, norm_gain.reshape(16, 128))
    return out.astype(bf16)


def solution(mesh):
    in_specs = (
        P(("qrow", "kcol"), None),
        P(("qrow", "kcol"), None),
        P(("qrow", "kcol"), None),
        P(),
        P(),
    )
    out_specs = P(("qrow", "kcol"), None)
    return jax.shard_map(shards, mesh=mesh, in_specs=in_specs, out_specs=out_specs, check_vma=False)
```

time: 27.9 us -> 24.7 us (0.89)
  Pallas kernels: 22.5 us -> 19.3 us
    pallas_call x1, Pallas kernels: 22.5 us -> 19.3 us  [shards(): pl.pallas_call(functools.partial(kernel, rows, cols, key_dev, heads), out...]
where the time goes in v2:
time: 24.7 us; the launch traced here: 24.4 us
  Pallas kernels  19.3 us (78%)
  local copies, waits for them, and re-layouts  4.5 us (18%)
  other arithmetic  0.61 us (2%)
    pallas_call x1, Pallas kernels, shards(): pl.pallas_call(functools.partial(kernel, rows, cols, key_dev, heads), out...  19.3 us
    unnamed x10, local copies, waits for them, and re-layouts  4.5 us
    convert_element_type x1, other arithmetic, shards(): return out.astype(bf16)  0.61 us

profile of v2, /device:TPU:0, one launch (start us, length us, event | category | flops | bytes accessed | tf_op | source)
XLA Modules:
  0.0 24.4 jit_solution(2776882140529526538)
XLA Ops:
  0.0 0.0 copy-start.4
  0.0 0.7 %copy-done.4 = f32[8]{0:T(128)S(1)} copy-done((f32[8]{0:T(128)S(1)}, f32[8]{0:T(128)}, u32[]{:S(2)}) %copy-start.4) | copy-done | bytes 56
  0.7 0.0 copy-start
  0.7 1.2 %copy-done = bf16[256,2048]{1,0:T(8,128)(2,1)S(1)} copy-done((bf16[256,2048]{1,0:T(8,128)(2,1)S(1)}, bf16[256,2048]{1,0:T(8,128)(2,1)}, u32[]{:S(2)}) %copy-start) | copy-done | bytes 1048600
  1.9 0.0 copy-start.1
  1.9 1.2 %copy-done.1 = bf16[256,2048]{1,0:T(8,128)(2,1)S(1)} copy-done((bf16[256,2048]{1,0:T(8,128)(2,1)S(1)}, bf16[256,2048]{1,0:T(8,128)(2,1)}, u32[]{:S(2)}) %copy-start.1) | copy-done | bytes 1048600
  3.1 0.0 copy-start.2
  3.1 0.7 %copy-done.2 = bf16[1,2048]{1,0:T(2,128)(2,1)S(1)} copy-done((bf16[1,2048]{1,0:T(2,128)(2,1)S(1)}, bf16[1,2048]{1,0:T(2,128)(2,1)}, u32[]{:S(2)}) %copy-start.2) | copy-done | bytes 4120
  3.8 0.0 copy-start.3
  3.8 0.7 %copy-done.3 = f32[2048]{0:T(1024)S(1)} copy-done((f32[2048]{0:T(1024)S(1)}, f32[2048]{0:T(1024)}, u32[]{:S(2)}) %copy-start.3) | copy-done | bytes 8216
  4.5 19.3 %shard_map.55 = f32[1,2048]{1,0:T(1,128)S(1)} custom-call(bf16[1,2048]{1,0:T(2,128)(2,1)S(1)} %copy-done.2, bf16[256,2048]{1,0:T(8,128)(2,1)S(1)} %copy-done, bf16[256,2048]{1,0:T(8,128)(2,1)S(1)} %copy-done.1, f32[8]{0:T(128)S(1)} %copy-done.4, f32[16,128]{1,0:T(8,128)S(1)} %bitcast.1), custom_call_target="tpu_custom_call" | custom-call | flops 100663296 | bytes 2097152 | tf_op jit(solution)/shard_map/pallas_call | solution.py:248
  23.8 0.6 %convert_element_type.3 = bf16[1,2048]{1,0:T(2,128)(2,1)} convert(f32[1,2048]{1,0:T(1,128)S(1)} %shard_map.55) | non-fusion elementwise | flops 2048 | bytes 12288 | tf_op jit(solution)/shard_map/convert_element_type | solution.py:282
Async XLA Ops:
  0.0 0.7 %copy-start.4 = (f32[8]{0:T(128)S(1)}, f32[8]{0:T(128)}, u32[]{:S(2)}) copy-start(f32[8]{0:T(128)} %lam_hbm.1) | copy-start | bytes 100
  0.7 1.2 %copy-start = (bf16[256,2048]{1,0:T(8,128)(2,1)S(1)}, bf16[256,2048]{1,0:T(8,128)(2,1)}, u32[]{:S(2)}) copy-start(bf16[256,2048]{1,0:T(8,128)(2,1)} %k_hbm.1) | copy-start | bytes 3145732
  1.9 1.2 %copy-start.1 = (bf16[256,2048]{1,0:T(8,128)(2,1)S(1)}, bf16[256,2048]{1,0:T(8,128)(2,1)}, u32[]{:S(2)}) copy-start(bf16[256,2048]{1,0:T(8,128)(2,1)} %v_hbm.1) | copy-start | bytes 3145732
  3.1 0.7 %copy-start.2 = (bf16[1,2048]{1,0:T(2,128)(2,1)S(1)}, bf16[1,2048]{1,0:T(2,128)(2,1)}, u32[]{:S(2)}) copy-start(bf16[1,2048]{1,0:T(2,128)(2,1)} %q_hbm.1) | copy-start | bytes 12292
  3.8 0.7 %copy-start.3 = (f32[2048]{0:T(1024)S(1)}, f32[2048]{0:T(1024)}, u32[]{:S(2)}) copy-start(f32[2048]{0:T(1024)} %param.9) | copy-start | bytes 24580

commit v3 on v2

--- a/solution.py
+++ b/solution.py
@@ -92,17 +92,17 @@
             src_ref=k_hbm.at[:, columns(1 - core, h)], dst_ref=k_buf.at[h, pl.ds(key_dev, key_dev)],
             send_sem=k_send.at[h], recv_sem=k_recv.at[h], device_id=sib, device_id_type=MESH))
         k_cross[-1].start()
-    for h in range(group):
-        v_cross.append(pltpu.make_async_remote_copy(
-            src_ref=v_hbm.at[:, columns(1 - core, h)], dst_ref=v_buf.at[h, pl.ds(key_dev, key_dev)],
-            send_sem=v_send.at[h], recv_sem=v_recv.at[h], device_id=sib, device_id_type=MESH))
-        v_cross[-1].start()
 
     q_cross.wait_recv()
     q_all[0] = q_pair[...].reshape(2 * maps, 128).astype(jnp.bfloat16)
     for_peers(lambda i: pltpu.make_async_remote_copy(
         src_ref=q_all.at[0], dst_ref=q_all.at[pairs - i], send_sem=qa_send, recv_sem=qa_recv,
         device_id=peer(i), device_id_type=MESH).start())
+    for h in range(group):
+        v_cross.append(pltpu.make_async_remote_copy(
+            src_ref=v_hbm.at[:, columns(1 - core, h)], dst_ref=v_buf.at[h, pl.ds(key_dev, key_dev)],
+            send_sem=v_send.at[h], recv_sem=v_recv.at[h], device_id=sib, device_id_type=MESH))
+        v_cross[-1].start()
 
     gain_copy.wait()
     for part in range(2):
@@ -275,7 +275,7 @@
             dma, dma, dma, dma, dma, dma, dma, dma, dma, dma,
         ],
         compiler_params=pltpu.CompilerParams(
-            collective_id=0, has_side_effects=True, vmem_limit_bytes=40 * 2**20),
+            collective_id=0, has_side_effects=True),
         cost_estimate=pl.CostEstimate(
             flops=6 * tall * 2 * key_dev * 1024, bytes_accessed=4 * key_dev * 2048, transcendentals=0),
     )(queries, key_maps, values, lambdas, norm_gain.reshape(16, 128))

time: 24.7 us -> 21.5 us (0.87)
  local copies, waits for them, and re-layouts: 4.5 us -> 0 us
  other arithmetic: 0.61 us -> 1.3 us
  Pallas kernels: 19.3 us -> 19.9 us
    unnamed x10 -> x0, local copies, waits for them, and re-layouts: 4.5 us -> none
    convert_element_type x1, other arithmetic: 0.61 us -> 1.3 us  [shards(): return out.astype(bf16)]
    pallas_call x1, Pallas kernels: 19.3 us -> 19.9 us  [shards(): pl.pallas_call(functools.partial(kernel, rows, cols, key_dev, heads), out...]
where the time goes in v3:
time: 21.5 us; the launch traced here: 21.2 us
  Pallas kernels  19.9 us (93%)
  other arithmetic  1.3 us (6%)
    pallas_call x1, Pallas kernels, shards(): pl.pallas_call(functools.partial(kernel, rows, cols, key_dev, heads), out...  19.9 us
    convert_element_type x1, other arithmetic, shards(): return out.astype(bf16)  1.3 us

profile of v3, /device:TPU:0, one launch (start us, length us, event | category | flops | bytes accessed | tf_op | source)
XLA Modules:
  0.0 21.2 jit_solution(10593072519770218594)
XLA Ops:
  0.0 19.9 %shard_map.55 = f32[1,2048]{1,0:T(1,128)} custom-call(bf16[1,2048]{1,0:T(2,128)(2,1)} %q_hbm.1, bf16[256,2048]{1,0:T(8,128)(2,1)} %k_hbm.1, bf16[256,2048]{1,0:T(8,128)(2,1)} %v_hbm.1, f32[8]{0:T(128)} %lam_hbm.1, f32[16,128]{1,0:T(8,128)} %bitcast.1), custom_call_target="tpu_custom_call" | custom-call | flops 100663296 | bytes 2097152 | tf_op jit(solution)/shard_map/pallas_call | solution.py:248
  19.9 1.3 %convert_element_type.3 = bf16[1,2048]{1,0:T(2,128)(2,1)} convert(f32[1,2048]{1,0:T(1,128)} %shard_map.55) | non-fusion elementwise | flops 2048 | bytes 12288 | tf_op jit(solution)/shard_map/convert_element_type | solution.py:282

commit v4 on v3

--- a/solution.py
+++ b/solution.py
@@ -17,9 +17,9 @@
     q_hbm, k_hbm, v_hbm, lam_hbm, gain_hbm,
     out_ref,
     q_own, lam_own, gain_own, k_buf, v_buf, q_split, q_pair, q_all, q_wide, bias,
-    stat_send, stat_recv, part_wide, part_send, part_recv, sum_pad, gain_rows, fin_send, fin_recv,
+    stat_send, stat_recv, part_wide, part_send, part_recv, sum_pad,
     q_sem, lam_sem, gain_sem, k_own_sem, v_own_sem, k_send, k_recv, v_send, v_recv,
-    qx_send, qx_recv, qa_send, qa_recv, st_send, st_recv, pa_send, pa_recv, fx_send, fx_recv,
+    qx_send, qx_recv, qa_send, qa_recv, st_send, st_recv, pa_send, pa_recv,
 ):
     row = lax.axis_index("qrow")
     col = lax.axis_index("kcol")
@@ -34,11 +34,11 @@
     tall = 2 * pairs
     keys = 2 * key_dev
 
-    def peer(offset):
+    def peer(offset, its_core):
         other = pair + offset
         other = jnp.where(other >= pairs, other - pairs, other)
         its_row = lax.div(other, half_cols)
-        return (its_row, 2 * (other - its_row * half_cols) + core)
+        return (its_row, 2 * (other - its_row * half_cols) + its_core)
 
     def for_peers(step):
         if pairs <= 16:
@@ -56,8 +56,13 @@
     q_copy = pltpu.make_async_copy(q_hbm, q_own, q_sem)
     q_copy.start()
     barrier = pltpu.get_barrier_semaphore()
-    for_peers(lambda i: pl.semaphore_signal(barrier, inc=1, device_id=peer(i), device_id_type=MESH))
+
+    def greet(i):
+        for j in range(2):
+            pl.semaphore_signal(barrier, inc=1, device_id=peer(i, j), device_id_type=MESH)
+
     pl.semaphore_signal(barrier, inc=1, device_id=sib, device_id_type=MESH)
+    for_peers(greet)
 
     lam_copy = pltpu.make_async_copy(lam_hbm, lam_own, lam_sem)
     lam_copy.start()
@@ -80,7 +85,7 @@
             q_split[g, m : m + 1, :] = q_own[:, at : at + 128].astype(jnp.float32)
     q_pair[core] = q_split[core]
 
-    pl.semaphore_wait(barrier, pairs)
+    pl.semaphore_wait(barrier, tall - 1)
 
     q_cross = pltpu.make_async_remote_copy(
         src_ref=q_split.at[1 - core], dst_ref=q_pair.at[core], send_sem=qx_send, recv_sem=qx_recv,
@@ -97,24 +102,19 @@
     q_all[0] = q_pair[...].reshape(2 * maps, 128).astype(jnp.bfloat16)
     for_peers(lambda i: pltpu.make_async_remote_copy(
         src_ref=q_all.at[0], dst_ref=q_all.at[pairs - i], send_sem=qa_send, recv_sem=qa_recv,
-        device_id=peer(i), device_id_type=MESH).start())
+        device_id=peer(i, core), device_id_type=MESH).start())
     for h in range(group):
         v_cross.append(pltpu.make_async_remote_copy(
             src_ref=v_hbm.at[:, columns(1 - core, h)], dst_ref=v_buf.at[h, pl.ds(key_dev, key_dev)],
             send_sem=v_send.at[h], recv_sem=v_recv.at[h], device_id=sib, device_id_type=MESH))
         v_cross[-1].start()
 
-    gain_copy.wait()
-    for part in range(2):
-        for h in range(group):
-            line = gain_own[pl.ds((core * group + h) * 2 + part, 1), :]
-            gain_rows[part, h : h + 1, :] = line
-            gain_rows[part, group + h : group + h + 1, :] = line
     lam_copy.wait()
     map_of = lax.broadcasted_iota(jnp.int32, (maps, tall), 0)
+    low = lax.broadcasted_iota(jnp.int32, (maps, tall), 1) < pairs
     sign = jnp.ones((maps, tall), jnp.float32)
     for h in range(group):
-        sign = jnp.where(map_of == 2 * h + 1, -lam_own[core * group + h], sign)
+        sign = jnp.where(map_of == 2 * h + 1, jnp.where(low, -lam_own[h], -lam_own[group + h]), sign)
 
     row_of = lax.broadcasted_iota(jnp.int32, (2 * tall, keys), 0)
     col_of = lax.broadcasted_iota(jnp.int32, (2 * tall, keys), 1)
@@ -154,10 +154,23 @@
             stats = jnp.where(lane == m, top[at], jnp.where(lane == maps + m, total[at], stats))
         expos.append(expo.astype(jnp.bfloat16))
     stat_send[...] = stats
-    for_peers(lambda i: pltpu.make_async_remote_copy(
-        src_ref=stat_send.at[pl.ds(2 * i, 2)], dst_ref=stat_recv.at[pl.ds(2 * i, 2)],
-        send_sem=st_send, recv_sem=st_recv, device_id=peer(i), device_id_type=MESH).start())
-    stat_recv[0:2] = stat_send[0:2]
+
+    def send_stats(t, where):
+        pltpu.make_async_remote_copy(
+            src_ref=stat_send.at[pl.ds(t, 1)], dst_ref=stat_recv.at[pl.ds(core * pairs + t // 2, 1)],
+            send_sem=st_send, recv_sem=st_recv, device_id=where, device_id_type=MESH).start()
+
+    def send_part(t, where):
+        pltpu.make_async_remote_copy(
+            src_ref=part_send.at[t], dst_ref=part_recv.at[t // 2 * 2 + core],
+            send_sem=pa_send, recv_sem=pa_recv, device_id=where, device_id_type=MESH).start()
+
+    def to_all(send):
+        for_peers(lambda i: [send(2 * i + j, peer(i, j)) for j in range(2)])
+        send(1 - core, sib)
+
+    to_all(send_stats)
+    stat_recv[pl.ds(core * pairs, 1)] = stat_send[pl.ds(core, 1)]
 
     for h in range(group):
         v_locals[h].wait()
@@ -166,69 +179,52 @@
         summed = jnp.dot(expos[h], v_buf[h], preferred_element_type=jnp.float32)
         for side in range(2):
             for part in range(2):
-                part_wide[part, pl.ds(2 * h + side, tall, stride=maps), :] = summed[
+                part_wide[pl.ds(part * maps + 2 * h + side, tall, stride=2 * maps), :] = summed[
                     side * tall : (side + 1) * tall, part * 128 : part * 128 + 128]
-    for part in range(2):
-        part_send[:, part] = part_wide[part].reshape(pairs, 2 * maps, 128).astype(jnp.bfloat16)
-    for_peers(lambda i: pltpu.make_async_remote_copy(
-        src_ref=part_send.at[i], dst_ref=part_recv.at[i], send_sem=pa_send, recv_sem=pa_recv,
-        device_id=peer(i), device_id_type=MESH).start())
-    part_recv[0] = part_send[0]
-
-    all_of(stat_recv.at[pl.ds(2, tall - 2)], st_recv)
+    part_send[...] = part_wide[...].reshape(tall, 2 * maps, 128).astype(jnp.bfloat16)
+    to_all(send_part)
+    part_recv[core] = part_send[core]
+
+    all_of(stat_recv.at[pl.ds(1, tall - 1)], st_recv)
     turned = stat_recv[...].T
     tops, totals = turned[0:maps], turned[maps : 2 * maps]
-    even = lax.rem(lax.broadcasted_iota(jnp.int32, (maps, tall), 1), 2) == 0
-
-    def per_query(array, reduce, fill):
-        zero = reduce(jnp.where(even, array, fill), axis=1, keepdims=True)
-        one = reduce(jnp.where(even, fill, array), axis=1, keepdims=True)
-        return jnp.where(even, zero, one)
-
-    factor = jnp.exp(tops - per_query(tops, jnp.max, -3e38))
-    factor = factor * sign / per_query(factor * totals, jnp.sum, 0.0)
-
-    all_of(part_recv.at[pl.ds(1, pairs - 1)], pa_recv)
+
+    def per_group(array, reduce, fill):
+        zero = reduce(jnp.where(low, array, fill), axis=1, keepdims=True)
+        one = reduce(jnp.where(low, fill, array), axis=1, keepdims=True)
+        return jnp.where(low, zero, one)
+
+    factor = jnp.exp(tops - per_group(tops, jnp.max, -3e38))
+    factor = factor * sign / per_group(factor * totals, jnp.sum, 0.0)
+    gain_copy.wait()
+
+    all_of(part_recv.at[pl.ds(1, tall - 1)], pa_recv)
     sums = [[jnp.zeros((maps, 128), jnp.float32) for _ in range(2)] for _ in range(2)]
     for s in range(pairs):
-        for part in range(2):
-            block = part_recv[s, part].astype(jnp.float32)
-            for j in range(2):
-                weight = factor[:, 2 * s + j : 2 * s + j + 1]
-                sums[part][j] = sums[part][j] + weight * block[j * maps : (j + 1) * maps]
+        for g in range(2):
+            weight = factor[:, g * pairs + s : g * pairs + s + 1]
+            block = part_recv[2 * s + g].astype(jnp.float32)
+            for part in range(2):
+                sums[part][g] = sums[part][g] + weight * block[part * maps : (part + 1) * maps]
     diffs = []
     for part in range(2):
-        for j in range(2):
-            sum_pad[part, j * maps : (j + 1) * maps] = sums[part][j]
+        for g in range(2):
+            sum_pad[part, g * maps : (g + 1) * maps] = sums[part][g]
         diffs.append(
-            sum_pad[part, pl.ds(0, maps, stride=2), :] + sum_pad[part, pl.ds(1, maps, stride=2), :])
+            sum_pad[part, pl.ds(0, heads, stride=2), :] + sum_pad[part, pl.ds(1, heads, stride=2), :])
     square = jnp.sum(diffs[0] * diffs[0] + diffs[1] * diffs[1], axis=1, keepdims=True) * (1.0 / 256)
     scale = jnp.sqrt(square + 1e-05)
-    for part in range(2):
-        normed = diffs[part] / scale * gain_rows[part]
-        for j in range(2):
-            fin_send[j, part * group : (part + 1) * group, :] = normed[j * group : (j + 1) * group]
-    fin_cross = pltpu.make_async_remote_copy(
-        src_ref=fin_send.at[1 - core], dst_ref=fin_recv, send_sem=fx_send, recv_sem=fx_recv,
-        device_id=sib, device_id_type=MESH)
-    fin_cross.start()
-
-    def put(which, lines):
-        for part in range(2):
-            for h in range(group):
-                at = pl.ds(pl.multiple_of(which * width + h * 256 + part * 128, 128), 128)
-                out_ref[:, at] = lines[part * group + h : part * group + h + 1]
-
-    put(core, fin_send[core])
+    normed = [diffs[part] / scale * gain_own[pl.ds(part, heads, stride=2), :] for part in range(2)]
+    line = jnp.concatenate([normed[part][h : h + 1] for h in range(heads) for part in range(2)], axis=1)
+    out_ref[...] = line.astype(jnp.bfloat16)
+
     q_cross.wait_send()
     for h in range(group):
         k_cross[h].wait_send()
         v_cross[h].wait_send()
     all_of(q_all.at[pl.ds(1, pairs - 1)], qa_send)
-    all_of(stat_send.at[pl.ds(2, tall - 2)], st_send)
-    all_of(part_send.at[pl.ds(1, pairs - 1)], pa_send)
-    fin_cross.wait()
-    put(1 - core, fin_recv[...])
+    all_of(stat_send.at[pl.ds(1, tall - 1)], st_send)
+    all_of(part_send.at[pl.ds(1, tall - 1)], pa_send)
 
 
 def shards(queries, key_maps, values, lambdas, norm_gain):
@@ -247,7 +243,7 @@
     in_hbm = pl.BlockSpec(memory_space=pltpu.HBM)
     out = pl.pallas_call(
         functools.partial(kernel, rows, cols, key_dev, heads),
-        out_shape=jax.ShapeDtypeStruct((1, 2048), f32),
+        out_shape=jax.ShapeDtypeStruct((1, 2048), bf16),
         in_specs=[in_hbm] * 5,
         out_specs=pl.BlockSpec(memory_space=pltpu.VMEM),
         scratch_shapes=[
@@ -263,23 +259,20 @@
             pltpu.VMEM((2 * tall, 2 * key_dev), f32),
             pltpu.VMEM((tall, 128), f32),
             pltpu.VMEM((tall, 128), f32),
-            pltpu.VMEM((2, pairs * 2 * maps, 128), f32),
-            pltpu.VMEM((pairs, 2, 2 * maps, 128), bf16),
-            pltpu.VMEM((pairs, 2, 2 * maps, 128), bf16),
+            pltpu.VMEM((tall * 2 * maps, 128), f32),
+            pltpu.VMEM((tall, 2 * maps, 128), bf16),
+            pltpu.VMEM((tall, 2 * maps, 128), bf16),
             pltpu.VMEM((2, 2 * maps, 128), f32),
-            pltpu.VMEM((2, 2 * group, 128), f32),
-            pltpu.VMEM((2, 2 * group, 128), f32),
-            pltpu.VMEM((2 * group, 128), f32),
             dma, dma, dma,
             dma((group,)), dma((group,)), dma((group,)), dma((group,)), dma((group,)), dma((group,)),
-            dma, dma, dma, dma, dma, dma, dma, dma, dma, dma,
+            dma, dma, dma, dma, dma, dma, dma, dma,
         ],
         compiler_params=pltpu.CompilerParams(
             collective_id=0, has_side_effects=True),
         cost_estimate=pl.CostEstimate(
             flops=6 * tall * 2 * key_dev * 1024, bytes_accessed=4 * key_dev * 2048, transcendentals=0),
     )(queries, key_maps, values, lambdas, norm_gain.reshape(16, 128))
-    return out.astype(bf16)
+    return out
 
 
 def solution(mesh):

time: 21.5 us -> 21.1 us (0.981)
  other arithmetic: 1.3 us -> 0 us
  local copies, waits for them, and re-layouts: 0 us -> 1.3 us
  Pallas kernels: 19.9 us -> 19.5 us
    unnamed x0 -> x1, local copies, waits for them, and re-layouts: none -> 1.3 us
    convert_element_type x1 -> x0, other arithmetic: 1.3 us -> none  [shards(): return out.astype(bf16)]
    pallas_call x1, Pallas kernels: 19.9 us -> 19.5 us  [shards(): pl.pallas_call(functools.partial(kernel, rows, cols, key_dev, heads), out...]
where the time goes in v4:
time: 21.1 us; the launch traced here: 20.8 us
  Pallas kernels  19.5 us (92%)
  local copies, waits for them, and re-layouts  1.3 us (6%)
    pallas_call x1, Pallas kernels, shards(): pl.pallas_call(functools.partial(kernel, rows, cols, key_dev, heads), out...  19.5 us
    unnamed x1, local copies, waits for them, and re-layouts  1.3 us

profile of v4, /device:TPU:0, one launch (start us, length us, event | category | flops | bytes accessed | tf_op | source)
XLA Modules:
  0.0 20.8 jit_solution(13027281168286686795)
XLA Ops:
  0.0 19.5 %shard_map.55 = bf16[1,2048]{1,0:T(2,128)(2,1)} custom-call(bf16[1,2048]{1,0:T(2,128)(2,1)} %q_hbm.1, bf16[256,2048]{1,0:T(8,128)(2,1)} %k_hbm.1, bf16[256,2048]{1,0:T(8,128)(2,1)} %v_hbm.1, f32[8]{0:T(128)} %lam_hbm.1, f32[16,128]{1,0:T(8,128)} %bitcast.1), custom_call_target="tpu_custom_call" | custom-call | flops 100663296 | bytes 2097152 | tf_op jit(solution)/shard_map/pallas_call | solution.py:244
  19.5 1.3 %copy.7 = bf16[1,2048]{1,0:T(2,128)(2,1)} copy(bf16[1,2048]{1,0:T(2,128)(2,1)} %shard_map.55) | data formatting | bytes 8192

commit v5 on v4

--- a/solution.py
+++ b/solution.py
@@ -16,10 +16,10 @@
     rows, cols, key_dev, heads,
     q_hbm, k_hbm, v_hbm, lam_hbm, gain_hbm,
     out_ref,
-    q_own, lam_own, gain_own, k_buf, v_buf, q_split, q_pair, q_all, q_wide, bias,
+    q_own, lam_own, gain_own, k_buf, v_buf, q_split, q_wide, bias,
     stat_send, stat_recv, part_wide, part_send, part_recv, sum_pad,
     q_sem, lam_sem, gain_sem, k_own_sem, v_own_sem, k_send, k_recv, v_send, v_recv,
-    qx_send, qx_recv, qa_send, qa_recv, st_send, st_recv, pa_send, pa_recv,
+    qa_send, qa_recv, st_send, st_recv, pa_send, pa_recv,
 ):
     row = lax.axis_index("qrow")
     col = lax.axis_index("kcol")
@@ -83,14 +83,21 @@
         for m in range(maps):
             at = (g * maps + m) * 128
             q_split[g, m : m + 1, :] = q_own[:, at : at + 128].astype(jnp.float32)
-    q_pair[core] = q_split[core]
+
+    def to_all(send):
+        for_peers(lambda i: [send(2 * i + j, peer(i, j), j) for j in range(2)])
+        send(1 - core, sib, 1 - core)
+
+    def send_query(t, where, its_core):
+        back = lax.rem(tall - (t - its_core), tall) + core
+        pltpu.make_async_remote_copy(
+            src_ref=q_split.at[its_core], dst_ref=q_wide.at[pl.ds(pl.multiple_of(back * maps, 8), maps)],
+            send_sem=qa_send, recv_sem=qa_recv, device_id=where, device_id_type=MESH).start()
 
     pl.semaphore_wait(barrier, tall - 1)
 
-    q_cross = pltpu.make_async_remote_copy(
-        src_ref=q_split.at[1 - core], dst_ref=q_pair.at[core], send_sem=qx_send, recv_sem=qx_recv,
-        device_id=sib, device_id_type=MESH)
-    q_cross.start()
+    to_all(send_query)
+    q_wide[pl.ds(pl.multiple_of(core * maps, 8), maps)] = q_split[core]
     k_cross, v_cross = [], []
     for h in range(group):
         k_cross.append(pltpu.make_async_remote_copy(
@@ -98,11 +105,6 @@
             send_sem=k_send.at[h], recv_sem=k_recv.at[h], device_id=sib, device_id_type=MESH))
         k_cross[-1].start()
 
-    q_cross.wait_recv()
-    q_all[0] = q_pair[...].reshape(2 * maps, 128).astype(jnp.bfloat16)
-    for_peers(lambda i: pltpu.make_async_remote_copy(
-        src_ref=q_all.at[0], dst_ref=q_all.at[pairs - i], send_sem=qa_send, recv_sem=qa_recv,
-        device_id=peer(i, core), device_id_type=MESH).start())
     for h in range(group):
         v_cross.append(pltpu.make_async_remote_copy(
             src_ref=v_hbm.at[:, columns(1 - core, h)], dst_ref=v_buf.at[h, pl.ds(key_dev, key_dev)],
@@ -131,8 +133,7 @@
     for h in range(group):
         k_locals[h].wait()
         k_cross[h].wait_recv()
-    all_of(q_all.at[pl.ds(1, pairs - 1)], qa_recv)
-    q_wide[...] = q_all[...].reshape(pairs * 2 * maps, 128).astype(jnp.float32)
+    all_of(q_wide.at[pl.ds(maps, (tall - 1) * maps)], qa_recv)
 
     stats = jnp.zeros((tall, 128), jnp.float32)
     expos = []
@@ -155,19 +156,15 @@
         expos.append(expo.astype(jnp.bfloat16))
     stat_send[...] = stats
 
-    def send_stats(t, where):
+    def send_stats(t, where, its_core):
         pltpu.make_async_remote_copy(
             src_ref=stat_send.at[pl.ds(t, 1)], dst_ref=stat_recv.at[pl.ds(core * pairs + t // 2, 1)],
             send_sem=st_send, recv_sem=st_recv, device_id=where, device_id_type=MESH).start()
 
-    def send_part(t, where):
+    def send_part(t, where, its_core):
         pltpu.make_async_remote_copy(
             src_ref=part_send.at[t], dst_ref=part_recv.at[t // 2 * 2 + core],
             send_sem=pa_send, recv_sem=pa_recv, device_id=where, device_id_type=MESH).start()
-
-    def to_all(send):
-        for_peers(lambda i: [send(2 * i + j, peer(i, j)) for j in range(2)])
-        send(1 - core, sib)
 
     to_all(send_stats)
     stat_recv[pl.ds(core * pairs, 1)] = stat_send[pl.ds(core, 1)]
@@ -218,11 +215,10 @@
     line = jnp.concatenate([normed[part][h : h + 1] for h in range(heads) for part in range(2)], axis=1)
     out_ref[...] = line.astype(jnp.bfloat16)
 
-    q_cross.wait_send()
     for h in range(group):
         k_cross[h].wait_send()
         v_cross[h].wait_send()
-    all_of(q_all.at[pl.ds(1, pairs - 1)], qa_send)
+    all_of(q_wide.at[pl.ds(maps, (tall - 1) * maps)], qa_send)
     all_of(stat_send.at[pl.ds(1, tall - 1)], st_send)
     all_of(part_send.at[pl.ds(1, tall - 1)], pa_send)
 
@@ -253,8 +249,6 @@
             pltpu.VMEM((group, 2 * key_dev, 256), bf16),
             pltpu.VMEM((group, 2 * key_dev, 256), bf16),
             pltpu.VMEM((2, maps, 128), f32),
-            pltpu.VMEM((2, maps, 128), f32),
-            pltpu.VMEM((pairs, 2 * maps, 128), bf16),
             pltpu.VMEM((pairs * 2 * maps, 128), f32),
             pltpu.VMEM((2 * tall, 2 * key_dev), f32),
             pltpu.VMEM((tall, 128), f32),
@@ -265,7 +259,7 @@
             pltpu.VMEM((2, 2 * maps, 128), f32),
             dma, dma, dma,
             dma((group,)), dma((group,)), dma((group,)), dma((group,)), dma((group,)), dma((group,)),
-            dma, dma, dma, dma, dma, dma, dma, dma,
+            dma, dma, dma, dma, dma, dma,
         ],
         compiler_params=pltpu.CompilerParams(
             collective_id=0, has_side_effects=True),

time: 21.1 us -> 21.3 us (level)
    pallas_call x1, Pallas kernels: 19.5 us -> 19.7 us  [shards(): pl.pallas_call(functools.partial(kernel, rows, cols, key_dev, heads), out...]
where the time goes in v5:
time: 21.3 us; the launch traced here: 21.1 us
  Pallas kernels  19.7 us (92%)
  local copies, waits for them, and re-layouts  1.3 us (6%)
    pallas_call x1, Pallas kernels, shards(): pl.pallas_call(functools.partial(kernel, rows, cols, key_dev, heads), out...  19.7 us
    unnamed x1, local copies, waits for them, and re-layouts  1.3 us

profile of v5, /device:TPU:0, one launch (start us, length us, event | category | flops | bytes accessed | tf_op | source)
XLA Modules:
  0.0 21.1 jit_solution(17158217919771370729)
XLA Ops:
  0.0 19.7 %shard_map.55 = bf16[1,2048]{1,0:T(2,128)(2,1)} custom-call(bf16[1,2048]{1,0:T(2,128)(2,1)} %q_hbm.1, bf16[256,2048]{1,0:T(8,128)(2,1)} %k_hbm.1, bf16[256,2048]{1,0:T(8,128)(2,1)} %v_hbm.1, f32[8]{0:T(128)} %lam_hbm.1, f32[16,128]{1,0:T(8,128)} %bitcast.1), custom_call_target="tpu_custom_call" | custom-call | flops 100663296 | bytes 2097152 | tf_op jit(solution)/shard_map/pallas_call | solution.py:240
  19.7 1.3 %copy.7 = bf16[1,2048]{1,0:T(2,128)(2,1)} copy(bf16[1,2048]{1,0:T(2,128)(2,1)} %shard_map.55) | data formatting | bytes 8192

commit v6 on v5

--- a/solution.py
+++ b/solution.py
@@ -16,7 +16,7 @@
     rows, cols, key_dev, heads,
     q_hbm, k_hbm, v_hbm, lam_hbm, gain_hbm,
     out_ref,
-    q_own, lam_own, gain_own, k_buf, v_buf, q_split, q_wide, bias,
+    q_own, lam_own, gain_own, k_buf, k_turned, v_buf, q_split, q_wide, bias,
     stat_send, stat_recv, part_wide, part_send, part_recv, sum_pad,
     q_sem, lam_sem, gain_sem, k_own_sem, v_own_sem, k_send, k_recv, v_send, v_recv,
     qa_send, qa_recv, st_send, st_recv, pa_send, pa_recv,
@@ -132,7 +132,10 @@
 
     for h in range(group):
         k_locals[h].wait()
+        k_turned[h, :, :key_dev] = k_buf[h, :key_dev].T
+    for h in range(group):
         k_cross[h].wait_recv()
+        k_turned[h, :, key_dev:] = k_buf[h, key_dev:].T
     all_of(q_wide.at[pl.ds(maps, (tall - 1) * maps)], qa_recv)
 
     stats = jnp.zeros((tall, 128), jnp.float32)
@@ -143,8 +146,7 @@
         second = q_wide[pl.ds(2 * h + 1, tall, stride=maps), :].astype(jnp.bfloat16)
         both = jnp.concatenate(
             [jnp.concatenate([first, blank], axis=1), jnp.concatenate([blank, second], axis=1)], axis=0)
-        score = lax.dot_general(
-            both, k_buf[h], (((1,), (1,)), ((), ())), preferred_element_type=jnp.float32)
+        score = jnp.dot(both, k_turned[h], preferred_element_type=jnp.float32)
         score = score * scaling + bias[...]
         top = jnp.max(score, axis=1, keepdims=True)
         expo = jnp.exp(score - top)
@@ -247,6 +249,7 @@
             pltpu.SMEM((heads,), f32),
             pltpu.VMEM((16, 128), f32),
             pltpu.VMEM((group, 2 * key_dev, 256), bf16),
+            pltpu.VMEM((group, 256, 2 * key_dev), bf16),
             pltpu.VMEM((group, 2 * key_dev, 256), bf16),
             pltpu.VMEM((2, maps, 128), f32),
             pltpu.VMEM((pairs * 2 * maps, 128), f32),

time: 21.3 us -> 21.2 us (level)
  no operation moved by 1% of the time
where the time goes in v6:
time: 21.2 us; the launch traced here: 20.9 us
  Pallas kernels  19.6 us (92%)
  local copies, waits for them, and re-layouts  1.3 us (6%)
    pallas_call x1, Pallas kernels, shards(): pl.pallas_call(functools.partial(kernel, rows, cols, key_dev, heads), out...  19.6 us
    unnamed x1, local copies, waits for them, and re-layouts  1.3 us

profile of v6, /device:TPU:0, one launch (start us, length us, event | category | flops | bytes accessed | tf_op | source)
XLA Modules:
  0.0 20.9 jit_solution(11568909955103334408)
XLA Ops:
  0.0 19.6 %shard_map.55 = bf16[1,2048]{1,0:T(2,128)(2,1)} custom-call(bf16[1,2048]{1,0:T(2,128)(2,1)} %q_hbm.1, bf16[256,2048]{1,0:T(8,128)(2,1)} %k_hbm.1, bf16[256,2048]{1,0:T(8,128)(2,1)} %v_hbm.1, f32[8]{0:T(128)} %lam_hbm.1, f32[16,128]{1,0:T(8,128)} %bitcast.1), custom_call_target="tpu_custom_call" | custom-call | flops 100663296 | bytes 2097152 | tf_op jit(solution)/shard_map/pallas_call | solution.py:242
  19.6 1.3 %copy.7 = bf16[1,2048]{1,0:T(2,128)(2,1)} copy(bf16[1,2048]{1,0:T(2,128)(2,1)} %shard_map.55) | data formatting | bytes 8192

commit v7 on v5

--- a/solution.py
+++ b/solution.py
@@ -16,7 +16,7 @@
     rows, cols, key_dev, heads,
     q_hbm, k_hbm, v_hbm, lam_hbm, gain_hbm,
     out_ref,
-    q_own, lam_own, gain_own, k_buf, v_buf, q_split, q_wide, bias,
+    q_own, lam_own, gain_own, k_buf, v_buf, q_split, q_msg, q_in, q_wide, bias,
     stat_send, stat_recv, part_wide, part_send, part_recv, sum_pad,
     q_sem, lam_sem, gain_sem, k_own_sem, v_own_sem, k_send, k_recv, v_send, v_recv,
     qa_send, qa_recv, st_send, st_recv, pa_send, pa_recv,
@@ -34,18 +34,34 @@
     tall = 2 * pairs
     keys = 2 * key_dev
 
-    def peer(offset, its_core):
-        other = pair + offset
-        other = jnp.where(other >= pairs, other - pairs, other)
+    half = pairs // 2
+
+    def apart(place):
+        return (place & 3) + 8 * ((place >> 2) & (half // 4 - 1)) + 4 * (1 - place // half)
+
+    def peer(place, its_core):
+        other = pair ^ apart(place)
         its_row = lax.div(other, half_cols)
         return (its_row, 2 * (other - its_row * half_cols) + its_core)
 
-    def for_peers(step):
+    def to_far(send):
         if pairs <= 16:
-            for i in range(1, pairs):
-                step(i)
+            for place in range(half):
+                for j in range(2):
+                    send(place, j, peer(place, j))
         else:
-            lax.fori_loop(1, pairs, lambda i, carry: (step(i), carry)[1], 0)
+            lax.fori_loop(0, half, lambda place, carry: ([
+                send(place, j, peer(place, j)) for j in range(2)], carry)[1], 0)
+
+    def to_near(send):
+        if pairs <= 16:
+            for place in range(half + 1, pairs):
+                for j in range(2):
+                    send(place, j, peer(place, j))
+        else:
+            lax.fori_loop(half + 1, pairs, lambda place, carry: ([
+                send(place, j, peer(place, j)) for j in range(2)], carry)[1], 0)
+        send(half, 1 - core, sib)
 
     def columns(which, h):
         return pl.ds(pl.multiple_of(which * width + h * 256, 128), 256)
@@ -57,12 +73,11 @@
     q_copy.start()
     barrier = pltpu.get_barrier_semaphore()
 
-    def greet(i):
-        for j in range(2):
-            pl.semaphore_signal(barrier, inc=1, device_id=peer(i, j), device_id_type=MESH)
-
-    pl.semaphore_signal(barrier, inc=1, device_id=sib, device_id_type=MESH)
-    for_peers(greet)
+    def greet(place, j, where):
+        pl.semaphore_signal(barrier, inc=1, device_id=where, device_id_type=MESH)
+
+    to_far(greet)
+    to_near(greet)
 
     lam_copy = pltpu.make_async_copy(lam_hbm, lam_own, lam_sem)
     lam_copy.start()
@@ -84,20 +99,18 @@
             at = (g * maps + m) * 128
             q_split[g, m : m + 1, :] = q_own[:, at : at + 128].astype(jnp.float32)
 
-    def to_all(send):
-        for_peers(lambda i: [send(2 * i + j, peer(i, j), j) for j in range(2)])
-        send(1 - core, sib, 1 - core)
-
-    def send_query(t, where, its_core):
-        back = lax.rem(tall - (t - its_core), tall) + core
+    q_msg[...] = q_split[...].astype(jnp.bfloat16)
+
+    def send_query(place, j, where):
         pltpu.make_async_remote_copy(
-            src_ref=q_split.at[its_core], dst_ref=q_wide.at[pl.ds(pl.multiple_of(back * maps, 8), maps)],
+            src_ref=q_msg.at[j], dst_ref=q_in.at[2 * place + core],
             send_sem=qa_send, recv_sem=qa_recv, device_id=where, device_id_type=MESH).start()
 
     pl.semaphore_wait(barrier, tall - 1)
 
-    to_all(send_query)
-    q_wide[pl.ds(pl.multiple_of(core * maps, 8), maps)] = q_split[core]
+    to_far(send_query)
+    to_near(send_query)
+    q_in[2 * half + core] = q_msg[core]
     k_cross, v_cross = [], []
     for h in range(group):
         k_cross.append(pltpu.make_async_remote_copy(
@@ -120,8 +133,10 @@
 
     row_of = lax.broadcasted_iota(jnp.int32, (2 * tall, keys), 0)
     col_of = lax.broadcasted_iota(jnp.int32, (2 * tall, keys), 1)
-    query = 2 * pair + jnp.where(row_of < tall, row_of, row_of - tall)
-    query = jnp.where(query >= tall, query - tall, query)
+    row_of = row_of & (tall - 1)
+    row_place = row_of >> 1
+    row_apart = (row_place & 3) + 8 * ((row_place >> 2) & (half // 4 - 1)) + jnp.where(row_place < half, 4, 0)
+    query = 2 * (pair ^ row_apart) + (row_of & 1)
     place = jnp.where(
         col_of < key_dev,
         (2 * pair + core) * key_dev + col_of,
@@ -133,7 +148,8 @@
     for h in range(group):
         k_locals[h].wait()
         k_cross[h].wait_recv()
-    all_of(q_wide.at[pl.ds(maps, (tall - 1) * maps)], qa_recv)
+    all_of(q_in.at[pl.ds(1, tall - 1)], qa_recv)
+    q_wide[...] = q_in[...].astype(jnp.float32).reshape(tall * maps, 128)
 
     stats = jnp.zeros((tall, 128), jnp.float32)
     expos = []
@@ -156,31 +172,38 @@
         expos.append(expo.astype(jnp.bfloat16))
     stat_send[...] = stats
 
-    def send_stats(t, where, its_core):
+    def send_stats(place, j, where):
         pltpu.make_async_remote_copy(
-            src_ref=stat_send.at[pl.ds(t, 1)], dst_ref=stat_recv.at[pl.ds(core * pairs + t // 2, 1)],
+            src_ref=stat_send.at[pl.ds(2 * place + j, 1)], dst_ref=stat_recv.at[pl.ds(core * pairs + place, 1)],
             send_sem=st_send, recv_sem=st_recv, device_id=where, device_id_type=MESH).start()
 
-    def send_part(t, where, its_core):
+    def send_part(place, j, where):
         pltpu.make_async_remote_copy(
-            src_ref=part_send.at[t], dst_ref=part_recv.at[t // 2 * 2 + core],
+            src_ref=part_send.at[2 * place + j], dst_ref=part_recv.at[2 * place + core],
             send_sem=pa_send, recv_sem=pa_recv, device_id=where, device_id_type=MESH).start()
 
-    to_all(send_stats)
-    stat_recv[pl.ds(core * pairs, 1)] = stat_send[pl.ds(core, 1)]
+    def weigh(start):
+        for h in range(group):
+            rows_of = jnp.concatenate([expos[h][start : start + pairs], expos[h][tall + start : tall + start + pairs]], axis=0)
+            summed = jnp.dot(rows_of, v_buf[h], preferred_element_type=jnp.float32)
+            for side in range(2):
+                for part in range(2):
+                    at = pl.ds(start * 2 * maps + part * maps + 2 * h + side, pairs, stride=2 * maps)
+                    part_wide[at, :] = summed[side * pairs : (side + 1) * pairs, part * 128 : part * 128 + 128]
+        part_send[start : start + pairs] = part_wide[start * 2 * maps : (start + pairs) * 2 * maps].reshape(
+            pairs, 2 * maps, 128).astype(jnp.bfloat16)
 
     for h in range(group):
         v_locals[h].wait()
         v_cross[h].wait_recv()
-    for h in range(group):
-        summed = jnp.dot(expos[h], v_buf[h], preferred_element_type=jnp.float32)
-        for side in range(2):
-            for part in range(2):
-                part_wide[pl.ds(part * maps + 2 * h + side, tall, stride=2 * maps), :] = summed[
-                    side * tall : (side + 1) * tall, part * 128 : part * 128 + 128]
-    part_send[...] = part_wide[...].reshape(tall, 2 * maps, 128).astype(jnp.bfloat16)
-    to_all(send_part)
-    part_recv[core] = part_send[core]
+    weigh(0)
+    to_far(send_part)
+    to_far(send_stats)
+    to_near(send_stats)
+    stat_recv[pl.ds(core * pairs + half, 1)] = stat_send[pl.ds(2 * half + core, 1)]
+    weigh(pairs)
+    to_near(send_part)
+    part_recv[2 * half + core] = part_send[2 * half + core]
 
     all_of(stat_recv.at[pl.ds(1, tall - 1)], st_recv)
     turned = stat_recv[...].T
@@ -218,7 +241,7 @@
     for h in range(group):
         k_cross[h].wait_send()
         v_cross[h].wait_send()
-    all_of(q_wide.at[pl.ds(maps, (tall - 1) * maps)], qa_send)
+    all_of(q_in.at[pl.ds(1, tall - 1)], qa_send)
     all_of(stat_send.at[pl.ds(1, tall - 1)], st_send)
     all_of(part_send.at[pl.ds(1, tall - 1)], pa_send)
 
@@ -229,7 +252,8 @@
     key_dev = key_maps.shape[0]
     assert queries.shape[0] == 1 and heads == 8
     assert key_maps.shape[1] == 2048 and values.shape[1] == 2048
-    assert cols % 2 == 0 and rows * cols <= 2 * key_dev
+    assert cols % 2 == 0 and rows * cols >= 16 and (rows * cols) & (rows * cols - 1) == 0
+    assert rows * cols <= 2 * key_dev
     group = heads // 2
     maps = 2 * group
     pairs = rows * cols // 2
@@ -249,7 +273,9 @@
             pltpu.VMEM((group, 2 * key_dev, 256), bf16),
             pltpu.VMEM((group, 2 * key_dev, 256), bf16),
             pltpu.VMEM((2, maps, 128), f32),
-            pltpu.VMEM((pairs * 2 * maps, 128), f32),
+            pltpu.VMEM((2, maps, 128), bf16),
+            pltpu.VMEM((tall, maps, 128), bf16),
+            pltpu.VMEM((tall * maps, 128), f32),
             pltpu.VMEM((2 * tall, 2 * key_dev), f32),
             pltpu.VMEM((tall, 128), f32),
             pltpu.VMEM((tall, 128), f32),

time: 21.3 us -> 21.4 us (level)
  no operation moved by 1% of the time
where the time goes in v7:
time: 21.4 us; the launch traced here: 21.2 us
  Pallas kernels  19.9 us (93%)
  local copies, waits for them, and re-layouts  1.3 us (6%)
    pallas_call x1, Pallas kernels, shards(): pl.pallas_call(functools.partial(kernel, rows, cols, key_dev, heads), out...  19.9 us
    unnamed x1, local copies, waits for them, and re-layouts  1.3 us

profile of v7, /device:TPU:0, one launch (start us, length us, event | category | flops | bytes accessed | tf_op | source)
XLA Modules:
  0.0 21.2 jit_solution(3112476696229853590)
XLA Ops:
  0.0 19.9 %shard_map.55 = bf16[1,2048]{1,0:T(2,128)(2,1)} custom-call(bf16[1,2048]{1,0:T(2,128)(2,1)} %q_hbm.1, bf16[256,2048]{1,0:T(8,128)(2,1)} %k_hbm.1, bf16[256,2048]{1,0:T(8,128)(2,1)} %v_hbm.1, f32[8]{0:T(128)} %lam_hbm.1, f32[16,128]{1,0:T(8,128)} %bitcast.1), custom_call_target="tpu_custom_call" | custom-call | flops 100663296 | bytes 2097152 | tf_op jit(solution)/shard_map/pallas_call | solution.py:264
  19.9 1.3 %copy.7 = bf16[1,2048]{1,0:T(2,128)(2,1)} copy(bf16[1,2048]{1,0:T(2,128)(2,1)} %shard_map.55) | data formatting | bytes 8192

commit v8 on v5

--- a/solution.py
+++ b/solution.py
@@ -16,7 +16,7 @@
     rows, cols, key_dev, heads,
     q_hbm, k_hbm, v_hbm, lam_hbm, gain_hbm,
     out_ref,
-    q_own, lam_own, gain_own, k_buf, v_buf, q_split, q_wide, bias,
+    q_own, lam_own, gain_own, k_buf, v_buf, q_split, q_msg, q_in, q_wide, bias,
     stat_send, stat_recv, part_wide, part_send, part_recv, sum_pad,
     q_sem, lam_sem, gain_sem, k_own_sem, v_own_sem, k_send, k_recv, v_send, v_recv,
     qa_send, qa_recv, st_send, st_recv, pa_send, pa_recv,
@@ -84,6 +84,8 @@
             at = (g * maps + m) * 128
             q_split[g, m : m + 1, :] = q_own[:, at : at + 128].astype(jnp.float32)
 
+    q_msg[...] = q_split[...].astype(jnp.bfloat16)
+
     def to_all(send):
         for_peers(lambda i: [send(2 * i + j, peer(i, j), j) for j in range(2)])
         send(1 - core, sib, 1 - core)
@@ -91,13 +93,13 @@
     def send_query(t, where, its_core):
         back = lax.rem(tall - (t - its_core), tall) + core
         pltpu.make_async_remote_copy(
-            src_ref=q_split.at[its_core], dst_ref=q_wide.at[pl.ds(pl.multiple_of(back * maps, 8), maps)],
+            src_ref=q_msg.at[its_core], dst_ref=q_in.at[back],
             send_sem=qa_send, recv_sem=qa_recv, device_id=where, device_id_type=MESH).start()
 
     pl.semaphore_wait(barrier, tall - 1)
 
     to_all(send_query)
-    q_wide[pl.ds(pl.multiple_of(core * maps, 8), maps)] = q_split[core]
+    q_in[core] = q_msg[core]
     k_cross, v_cross = [], []
     for h in range(group):
         k_cross.append(pltpu.make_async_remote_copy(
@@ -133,7 +135,8 @@
     for h in range(group):
         k_locals[h].wait()
         k_cross[h].wait_recv()
-    all_of(q_wide.at[pl.ds(maps, (tall - 1) * maps)], qa_recv)
+    all_of(q_in.at[pl.ds(1, tall - 1)], qa_recv)
+    q_wide[...] = q_in[...].astype(jnp.float32).reshape(tall * maps, 128)
 
     stats = jnp.zeros((tall, 128), jnp.float32)
     expos = []
@@ -218,7 +221,7 @@
     for h in range(group):
         k_cross[h].wait_send()
         v_cross[h].wait_send()
-    all_of(q_wide.at[pl.ds(maps, (tall - 1) * maps)], qa_send)
+    all_of(q_in.at[pl.ds(1, tall - 1)], qa_send)
     all_of(stat_send.at[pl.ds(1, tall - 1)], st_send)
     all_of(part_send.at[pl.ds(1, tall - 1)], pa_send)
 
@@ -249,7 +252,9 @@
             pltpu.VMEM((group, 2 * key_dev, 256), bf16),
             pltpu.VMEM((group, 2 * key_dev, 256), bf16),
             pltpu.VMEM((2, maps, 128), f32),
-            pltpu.VMEM((pairs * 2 * maps, 128), f32),
+            pltpu.VMEM((2, maps, 128), bf16),
+            pltpu.VMEM((tall, maps, 128), bf16),
+            pltpu.VMEM((tall * maps, 128), f32),
             pltpu.VMEM((2 * tall, 2 * key_dev), f32),
             pltpu.VMEM((tall, 128), f32),
             pltpu.VMEM((tall, 128), f32),

time: 21.3 us -> 20.3 us (0.953)
  Pallas kernels: 19.7 us -> 18.7 us
    pallas_call x1, Pallas kernels: 19.7 us -> 18.7 us  [shards(): pl.pallas_call(functools.partial(kernel, rows, cols, key_dev, heads), out...]
where the time goes in v8:
time: 20.3 us; the launch traced here: 20 us
  Pallas kernels  18.7 us (92%)
  local copies, waits for them, and re-layouts  1.3 us (6%)
    pallas_call x1, Pallas kernels, shards(): pl.pallas_call(functools.partial(kernel, rows, cols, key_dev, heads), out...  18.7 us
    unnamed x1, local copies, waits for them, and re-layouts  1.3 us

profile of v8, /device:TPU:0, one launch (start us, length us, event | category | flops | bytes accessed | tf_op | source)
XLA Modules:
  0.0 20.0 jit_solution(9282885965272924877)
XLA Ops:
  0.0 18.7 %shard_map.55 = bf16[1,2048]{1,0:T(2,128)(2,1)} custom-call(bf16[1,2048]{1,0:T(2,128)(2,1)} %q_hbm.1, bf16[256,2048]{1,0:T(8,128)(2,1)} %k_hbm.1, bf16[256,2048]{1,0:T(8,128)(2,1)} %v_hbm.1, f32[8]{0:T(128)} %lam_hbm.1, f32[16,128]{1,0:T(8,128)} %bitcast.1), custom_call_target="tpu_custom_call" | custom-call | flops 100663296 | bytes 2097152 | tf_op jit(solution)/shard_map/pallas_call | solution.py:243
  18.7 1.3 %copy.7 = bf16[1,2048]{1,0:T(2,128)(2,1)} copy(bf16[1,2048]{1,0:T(2,128)(2,1)} %shard_map.55) | data formatting | bytes 8192

commit v9 on v8

--- a/solution.py
+++ b/solution.py
@@ -14,11 +14,11 @@
 
 def kernel(
     rows, cols, key_dev, heads,
-    q_hbm, k_hbm, v_hbm, lam_hbm, gain_hbm,
+    q_hbm, k_hbm, v_hbm, lam_hbm,
     out_ref,
-    q_own, lam_own, gain_own, k_buf, v_buf, q_split, q_msg, q_in, q_wide, bias,
+    q_own, lam_own, k_buf, v_buf, q_split, q_msg, q_in, q_wide, bias,
     stat_send, stat_recv, part_wide, part_send, part_recv, sum_pad,
-    q_sem, lam_sem, gain_sem, k_own_sem, v_own_sem, k_send, k_recv, v_send, v_recv,
+    q_sem, lam_sem, k_own_sem, v_own_sem, k_send, k_recv, v_send, v_recv,
     qa_send, qa_recv, st_send, st_recv, pa_send, pa_recv,
 ):
     row = lax.axis_index("qrow")
@@ -66,8 +66,6 @@
 
     lam_copy = pltpu.make_async_copy(lam_hbm, lam_own, lam_sem)
     lam_copy.start()
-    gain_copy = pltpu.make_async_copy(gain_hbm, gain_own, gain_sem)
-    gain_copy.start()
     k_locals, v_locals = [], []
     for h in range(group):
         k_locals.append(pltpu.make_async_copy(
@@ -196,7 +194,6 @@
 
     factor = jnp.exp(tops - per_group(tops, jnp.max, -3e38))
     factor = factor * sign / per_group(factor * totals, jnp.sum, 0.0)
-    gain_copy.wait()
 
     all_of(part_recv.at[pl.ds(1, tall - 1)], pa_recv)
     sums = [[jnp.zeros((maps, 128), jnp.float32) for _ in range(2)] for _ in range(2)]
@@ -214,9 +211,9 @@
             sum_pad[part, pl.ds(0, heads, stride=2), :] + sum_pad[part, pl.ds(1, heads, stride=2), :])
     square = jnp.sum(diffs[0] * diffs[0] + diffs[1] * diffs[1], axis=1, keepdims=True) * (1.0 / 256)
     scale = jnp.sqrt(square + 1e-05)
-    normed = [diffs[part] / scale * gain_own[pl.ds(part, heads, stride=2), :] for part in range(2)]
+    normed = [diffs[part] / scale for part in range(2)]
     line = jnp.concatenate([normed[part][h : h + 1] for h in range(heads) for part in range(2)], axis=1)
-    out_ref[...] = line.astype(jnp.bfloat16)
+    out_ref[...] = line
 
     for h in range(group):
         k_cross[h].wait_send()
@@ -242,13 +239,12 @@
     in_hbm = pl.BlockSpec(memory_space=pltpu.HBM)
     out = pl.pallas_call(
         functools.partial(kernel, rows, cols, key_dev, heads),
-        out_shape=jax.ShapeDtypeStruct((1, 2048), bf16),
-        in_specs=[in_hbm] * 5,
+        out_shape=jax.ShapeDtypeStruct((1, 2048), f32),
+        in_specs=[in_hbm] * 4,
         out_specs=pl.BlockSpec(memory_space=pltpu.VMEM),
         scratch_shapes=[
             pltpu.VMEM((1, 2048), bf16),
             pltpu.SMEM((heads,), f32),
-            pltpu.VMEM((16, 128), f32),
             pltpu.VMEM((group, 2 * key_dev, 256), bf16),
             pltpu.VMEM((group, 2 * key_dev, 256), bf16),
             pltpu.VMEM((2, maps, 128), f32),
@@ -262,16 +258,16 @@
             pltpu.VMEM((tall, 2 * maps, 128), bf16),
             pltpu.VMEM((tall, 2 * maps, 128), bf16),
             pltpu.VMEM((2, 2 * maps, 128), f32),
-            dma, dma, dma,
+            dma, dma,
             dma((group,)), dma((group,)), dma((group,)), dma((group,)), dma((group,)), dma((group,)),
             dma, dma, dma, dma, dma, dma,
         ],
         compiler_params=pltpu.CompilerParams(
-            collective_id=0, has_side_effects=True),
+            collective_id=0, has_side_effects=True, vmem_limit_bytes=53 * 2**20),
         cost_estimate=pl.CostEstimate(
             flops=6 * tall * 2 * key_dev * 1024, bytes_accessed=4 * key_dev * 2048, transcendentals=0),
-    )(queries, key_maps, values, lambdas, norm_gain.reshape(16, 128))
-    return out
+    )(queries, key_maps, values, lambdas)
+    return (out * norm_gain[None, :]).astype(bf16)
 
 
 def solution(mesh):

time: 20.3 us -> 20.3 us (level)
  other arithmetic: 0 us -> 0.61 us
  Pallas kernels: 18.7 us -> 18.1 us
    convert_element_type x0 -> x1, other arithmetic: none -> 0.61 us  [shards(): return (out * norm_gain[None, :]).astype(bf16)]
    pallas_call x1, Pallas kernels: 18.7 us -> 18.1 us  [shards(): pl.pallas_call(functools.partial(kernel, rows, cols, key_dev, heads), out...]
    unnamed x1 -> x6, local copies, waits for them, and re-layouts: 1.3 us -> 1.35 us
where the time goes in v9:
time: 20.3 us; the launch traced here: 20.1 us
  Pallas kernels  18.1 us (89%)
  local copies, waits for them, and re-layouts  1.35 us (7%)
  other arithmetic  0.61 us (3%)
    pallas_call x1, Pallas kernels, shards(): pl.pallas_call(functools.partial(kernel, rows, cols, key_dev, heads), out...  18.1 us
    unnamed x6, local copies, waits for them, and re-layouts  1.35 us
    convert_element_type x1, other arithmetic, shards(): return (out * norm_gain[None, :]).astype(bf16)  0.61 us

profile of v9, /device:TPU:0, one launch (start us, length us, event | category | flops | bytes accessed | tf_op | source)
XLA Modules:
  0.0 20.1 jit_solution(130760308979210143)
XLA Ops:
  0.0 0.0 copy-start.1
  0.0 0.7 %copy-done.1 = f32[8]{0:T(128)S(1)} copy-done((f32[8]{0:T(128)S(1)}, f32[8]{0:T(128)}, u32[]{:S(2)}) %copy-start.1) | copy-done | bytes 56
  0.7 0.0 copy-start
  0.7 0.7 %copy-done = bf16[1,2048]{1,0:T(2,128)(2,1)S(1)} copy-done((bf16[1,2048]{1,0:T(2,128)(2,1)S(1)}, bf16[1,2048]{1,0:T(2,128)(2,1)}, u32[]{:S(2)}) %copy-start) | copy-done | bytes 4120
  1.4 0.0 copy-start.2
  1.4 18.1 %shard_map.55 = f32[1,2048]{1,0:T(1,128)S(1)} custom-call(bf16[1,2048]{1,0:T(2,128)(2,1)S(1)} %copy-done, bf16[256,2048]{1,0:T(8,128)(2,1)} %k_hbm.1, bf16[256,2048]{1,0:T(8,128)(2,1)} %v_hbm.1, f32[8]{0:T(128)S(1)} %copy-done.1), custom_call_target="tpu_custom_call" | custom-call | flops 100663296 | bytes 2097152 | tf_op jit(solution)/shard_map/pallas_call | solution.py:240
  19.5 0.0 copy-done.2
  19.5 0.6 %multiply_convert_fusion = bf16[1,2048]{1,0:T(2,128)(2,1)} fusion(f32[1,2048]{1,0:T(1,128)S(1)} %shard_map.55, f32[1,2048]{1,0:T(1,128)S(1)} %bitcast.1), kind=kLoop, calls=%fused_computation | loop fusion | flops 4096 | bytes 20480 | tf_op jit(solution)/shard_map/convert_element_type | solution.py:270
Async XLA Ops:
  0.0 0.7 %copy-start.1 = (f32[8]{0:T(128)S(1)}, f32[8]{0:T(128)}, u32[]{:S(2)}) copy-start(f32[8]{0:T(128)} %lam_hbm.1) | copy-start | bytes 100
  0.7 0.7 %copy-start = (bf16[1,2048]{1,0:T(2,128)(2,1)S(1)}, bf16[1,2048]{1,0:T(2,128)(2,1)}, u32[]{:S(2)}) copy-start(bf16[1,2048]{1,0:T(2,128)(2,1)} %q_hbm.1) | copy-start | bytes 12292
  1.4 18.1 %copy-start.2 = (f32[2048]{0:T(1024)S(1)}, f32[2048]{0:T(1024)}, u32[]{:S(2)}) copy-start(f32[2048]{0:T(1024)} %param.9) | copy-start | bytes 24580

commit v10 on v9

--- a/solution.py
+++ b/solution.py
@@ -263,7 +263,7 @@
             dma, dma, dma, dma, dma, dma,
         ],
         compiler_params=pltpu.CompilerParams(
-            collective_id=0, has_side_effects=True, vmem_limit_bytes=53 * 2**20),
+            collective_id=0, has_side_effects=True, vmem_limit_bytes=54 * 2**20 - 80 * 2**10),
         cost_estimate=pl.CostEstimate(
             flops=6 * tall * 2 * key_dev * 1024, bytes_accessed=4 * key_dev * 2048, transcendentals=0),
     )(queries, key_maps, values, lambdas)

time: 20.3 us -> 19.5 us (0.961)
  local copies, waits for them, and re-layouts: 1.35 us -> 0.66 us
    unnamed x6 -> x4, local copies, waits for them, and re-layouts: 1.35 us -> 0.66 us
where the time goes in v10:
time: 19.5 us; the launch traced here: 19.4 us
  Pallas kernels  18.1 us (93%)
  local copies, waits for them, and re-layouts  0.66 us (3%)
  other arithmetic  0.61 us (3%)
    pallas_call x1, Pallas kernels, shards(): pl.pallas_call(functools.partial(kernel, rows, cols, key_dev, heads), out...  18.1 us
    unnamed x4, local copies, waits for them, and re-layouts  0.66 us
    convert_element_type x1, other arithmetic, shards(): return (out * norm_gain[None, :]).astype(bf16)  0.61 us

profile of v10, /device:TPU:0, one launch (start us, length us, event | category | flops | bytes accessed | tf_op | source)
XLA Modules:
  0.0 19.4 jit_solution(5734390554310971812)
XLA Ops:
  0.0 0.0 copy-start
  0.0 0.7 %copy-done = f32[8]{0:T(128)S(1)} copy-done((f32[8]{0:T(128)S(1)}, f32[8]{0:T(128)}, u32[]{:S(2)}) %copy-start) | copy-done | bytes 56
  0.7 0.0 copy-start.1
  0.7 18.1 %shard_map.55 = f32[1,2048]{1,0:T(1,128)S(1)} custom-call(bf16[1,2048]{1,0:T(2,128)(2,1)} %q_hbm.1, bf16[256,2048]{1,0:T(8,128)(2,1)} %k_hbm.1, bf16[256,2048]{1,0:T(8,128)(2,1)} %v_hbm.1, f32[8]{0:T(128)S(1)} %copy-done), custom_call_target="tpu_custom_call" | custom-call | flops 100663296 | bytes 2097152 | tf_op jit(solution)/shard_map/pallas_call | solution.py:240
  18.8 0.0 copy-done.1
  18.8 0.6 %multiply_convert_fusion = bf16[1,2048]{1,0:T(2,128)(2,1)} fusion(f32[1,2048]{1,0:T(1,128)S(1)} %shard_map.55, f32[1,2048]{1,0:T(1,128)S(1)} %bitcast.1), kind=kLoop, calls=%fused_computation | loop fusion | flops 4096 | bytes 20480 | tf_op jit(solution)/shard_map/convert_element_type | solution.py:270
Async XLA Ops:
  0.0 0.7 %copy-start = (f32[8]{0:T(128)S(1)}, f32[8]{0:T(128)}, u32[]{:S(2)}) copy-start(f32[8]{0:T(128)} %lam_hbm.1) | copy-start | bytes 100
  0.7 18.1 %copy-start.1 = (f32[2048]{0:T(1024)S(1)}, f32[2048]{0:T(1024)}, u32[]{:S(2)}) copy-start(f32[2048]{0:T(1024)} %param.9) | copy-start | bytes 24580

commit v11 on v10

--- a/solution.py
+++ b/solution.py
@@ -40,12 +40,12 @@
         its_row = lax.div(other, half_cols)
         return (its_row, 2 * (other - its_row * half_cols) + its_core)
 
-    def for_peers(step):
+    def for_peers(step, first=1, last=pairs):
         if pairs <= 16:
-            for i in range(1, pairs):
+            for i in range(first, last):
                 step(i)
         else:
-            lax.fori_loop(1, pairs, lambda i, carry: (step(i), carry)[1], 0)
+            lax.fori_loop(first, last, lambda i, carry: (step(i), carry)[1], 0)
 
     def columns(which, h):
         return pl.ds(pl.multiple_of(which * width + h * 256, 128), 256)
@@ -173,14 +173,24 @@
     for h in range(group):
         v_locals[h].wait()
         v_cross[h].wait_recv()
-    for h in range(group):
-        summed = jnp.dot(expos[h], v_buf[h], preferred_element_type=jnp.float32)
-        for side in range(2):
-            for part in range(2):
-                part_wide[pl.ds(part * maps + 2 * h + side, tall, stride=2 * maps), :] = summed[
-                    side * tall : (side + 1) * tall, part * 128 : part * 128 + 128]
-    part_send[...] = part_wide[...].reshape(tall, 2 * maps, 128).astype(jnp.bfloat16)
-    to_all(send_part)
+    def weigh(start):
+        for h in range(group):
+            weights = jnp.concatenate(
+                [expos[h][start : start + pairs], expos[h][tall + start : tall + start + pairs]], axis=0)
+            summed = jnp.dot(weights, v_buf[h], preferred_element_type=jnp.float32)
+            for side in range(2):
+                for part in range(2):
+                    at = pl.ds(start * 2 * maps + part * maps + 2 * h + side, pairs, stride=2 * maps)
+                    part_wide[at, :] = summed[side * pairs : (side + 1) * pairs, part * 128 : part * 128 + 128]
+        part_send[start : start + pairs] = part_wide[start * 2 * maps : (start + pairs) * 2 * maps].reshape(
+            pairs, 2 * maps, 128).astype(jnp.bfloat16)
+
+    middle = pairs // 2
+    weigh(0)
+    for_peers(lambda i: [send_part(2 * i + j, peer(i, j), j) for j in range(2)], 1, middle)
+    weigh(pairs)
+    for_peers(lambda i: [send_part(2 * i + j, peer(i, j), j) for j in range(2)], middle, pairs)
+    send_part(1 - core, sib, 1 - core)
     part_recv[core] = part_send[core]
 
     all_of(stat_recv.at[pl.ds(1, tall - 1)], st_recv)

time: 19.5 us -> 19.5 us (level)
  no operation moved by 1% of the time
where the time goes in v11:
time: 19.5 us; the launch traced here: 19.4 us
  Pallas kernels  18.1 us (93%)
  local copies, waits for them, and re-layouts  0.66 us (3%)
  other arithmetic  0.61 us (3%)
    pallas_call x1, Pallas kernels, shards(): pl.pallas_call(functools.partial(kernel, rows, cols, key_dev, heads), out...  18.1 us
    unnamed x4, local copies, waits for them, and re-layouts  0.66 us
    convert_element_type x1, other arithmetic, shards(): return (out * norm_gain[None, :]).astype(bf16)  0.61 us

profile of v11, /device:TPU:0, one launch (start us, length us, event | category | flops | bytes accessed | tf_op | source)
XLA Modules:
  0.0 19.4 jit_solution(7320394150862289955)
XLA Ops:
  0.0 0.0 copy-start
  0.0 0.7 %copy-done = f32[8]{0:T(128)S(1)} copy-done((f32[8]{0:T(128)S(1)}, f32[8]{0:T(128)}, u32[]{:S(2)}) %copy-start) | copy-done | bytes 56
  0.7 0.0 copy-start.1
  0.7 18.1 %shard_map.55 = f32[1,2048]{1,0:T(1,128)S(1)} custom-call(bf16[1,2048]{1,0:T(2,128)(2,1)} %q_hbm.1, bf16[256,2048]{1,0:T(8,128)(2,1)} %k_hbm.1, bf16[256,2048]{1,0:T(8,128)(2,1)} %v_hbm.1, f32[8]{0:T(128)S(1)} %copy-done), custom_call_target="tpu_custom_call" | custom-call | flops 100663296 | bytes 2097152 | tf_op jit(solution)/shard_map/pallas_call | solution.py:250
  18.7 0.0 copy-done.1
  18.7 0.6 %multiply_convert_fusion = bf16[1,2048]{1,0:T(2,128)(2,1)} fusion(f32[1,2048]{1,0:T(1,128)S(1)} %shard_map.55, f32[1,2048]{1,0:T(1,128)S(1)} %bitcast.1), kind=kLoop, calls=%fused_computation | loop fusion | flops 4096 | bytes 20480 | tf_op jit(solution)/shard_map/convert_element_type | solution.py:280
Async XLA Ops:
  0.0 0.7 %copy-start = (f32[8]{0:T(128)S(1)}, f32[8]{0:T(128)}, u32[]{:S(2)}) copy-start(f32[8]{0:T(128)} %lam_hbm.1) | copy-start | bytes 100
  0.7 18.1 %copy-start.1 = (f32[2048]{0:T(1024)S(1)}, f32[2048]{0:T(1024)}, u32[]{:S(2)}) copy-start(f32[2048]{0:T(1024)} %param.9) | copy-start | bytes 24580

commit v12 on v11

--- a/solution.py
+++ b/solution.py
@@ -167,8 +167,6 @@
             src_ref=part_send.at[t], dst_ref=part_recv.at[t // 2 * 2 + core],
             send_sem=pa_send, recv_sem=pa_recv, device_id=where, device_id_type=MESH).start()
 
-    to_all(send_stats)
-    stat_recv[pl.ds(core * pairs, 1)] = stat_send[pl.ds(core, 1)]
 
     for h in range(group):
         v_locals[h].wait()
@@ -188,6 +186,8 @@
     middle = pairs // 2
     weigh(0)
     for_peers(lambda i: [send_part(2 * i + j, peer(i, j), j) for j in range(2)], 1, middle)
+    to_all(send_stats)
+    stat_recv[pl.ds(core * pairs, 1)] = stat_send[pl.ds(core, 1)]
     weigh(pairs)
     for_peers(lambda i: [send_part(2 * i + j, peer(i, j), j) for j in range(2)], middle, pairs)
     send_part(1 - core, sib, 1 - core)

time: 19.5 us -> 20.3 us (1.041)
  Pallas kernels: 18.1 us -> 18.8 us
    pallas_call x1, Pallas kernels: 18.1 us -> 18.8 us  [shards(): pl.pallas_call(functools.partial(kernel, rows, cols, key_dev, heads), out...]
where the time goes in v12:
time: 20.3 us; the launch traced here: 20.1 us
  Pallas kernels  18.8 us (93%)
  local copies, waits for them, and re-layouts  0.66 us (3%)
  other arithmetic  0.61 us (3%)
    pallas_call x1, Pallas kernels, shards(): pl.pallas_call(functools.partial(kernel, rows, cols, key_dev, heads), out...  18.8 us
    unnamed x4, local copies, waits for them, and re-layouts  0.66 us
    convert_element_type x1, other arithmetic, shards(): return (out * norm_gain[None, :]).astype(bf16)  0.61 us

profile of v12, /device:TPU:0, one launch (start us, length us, event | category | flops | bytes accessed | tf_op | source)
XLA Modules:
  0.0 20.1 jit_solution(17420558408672714153)
XLA Ops:
  0.0 0.0 copy-start
  0.0 0.7 %copy-done = f32[8]{0:T(128)S(1)} copy-done((f32[8]{0:T(128)S(1)}, f32[8]{0:T(128)}, u32[]{:S(2)}) %copy-start) | copy-done | bytes 56
  0.7 0.0 copy-start.1
  0.7 18.8 %shard_map.55 = f32[1,2048]{1,0:T(1,128)S(1)} custom-call(bf16[1,2048]{1,0:T(2,128)(2,1)} %q_hbm.1, bf16[256,2048]{1,0:T(8,128)(2,1)} %k_hbm.1, bf16[256,2048]{1,0:T(8,128)(2,1)} %v_hbm.1, f32[8]{0:T(128)S(1)} %copy-done), custom_call_target="tpu_custom_call" | custom-call | flops 100663296 | bytes 2097152 | tf_op jit(solution)/shard_map/pallas_call | solution.py:250
  19.5 0.0 copy-done.1
  19.5 0.6 %multiply_convert_fusion = bf16[1,2048]{1,0:T(2,128)(2,1)} fusion(f32[1,2048]{1,0:T(1,128)S(1)} %shard_map.55, f32[1,2048]{1,0:T(1,128)S(1)} %bitcast.1), kind=kLoop, calls=%fused_computation | loop fusion | flops 4096 | bytes 20480 | tf_op jit(solution)/shard_map/convert_element_type | solution.py:280
Async XLA Ops:
  0.0 0.7 %copy-start = (f32[8]{0:T(128)S(1)}, f32[8]{0:T(128)}, u32[]{:S(2)}) copy-start(f32[8]{0:T(128)} %lam_hbm.1) | copy-start | bytes 100
  0.7 18.8 %copy-start.1 = (f32[2048]{0:T(1024)S(1)}, f32[2048]{0:T(1024)}, u32[]{:S(2)}) copy-start(f32[2048]{0:T(1024)} %param.9) | copy-start | bytes 24580
